TPU v7x, 256 devices: a whole 4x4x8 slice. The times are simulated.
256 devices in a mesh: gx: 64 (over y, z, x_hi), gy: 4 (over x_lo, core).
Axes of the slice: x: 4 (x_hi: 2, x_lo: 2; x = x_hi * 2 + x_lo), y: 4, z: 8, core: 2. Of those that a mesh axis runs over, the one named last changes fastest.
Arguments:
- positions: float32 [3, 64, 4, 128], P(None, 'gx', 'gy'), may hold values from 0 to 1
- atom_features: float32 [64, 4, 128, 128], P('gx', 'gy'), may hold values from -6 to 6
- atom_count: int32 [64, 4], P('gx', 'gy'), may hold values from 80 to 128, as said below
- edge_count: int32 [64, 4], P('gx', 'gy'), may hold values from 192 to 512, as said below
- centers: int32 [64, 4, 512], P('gx', 'gy'), may hold values from 0 to 127, as said below
- neighbours: int32 [64, 4, 512], P('gx', 'gy'), may hold values from 0 to 303, as said below
- send_across: int32 [64, 4, 2, 64], P('gx', 'gy'), may hold values from 0 to 127, as said below
- send_along: int32 [64, 4, 2, 16], P('gx', 'gy'), may hold values from 0 to 127, as said below
- send_corner: int32 [64, 4, 4, 4], P('gx', 'gy'), may hold values from 0 to 127, as said below
- radial_weight: float32 [8, 128], replicated, may hold values from -2 to 2
- pair_weight: float32 [2, 128, 128], replicated, may hold values from -0.5 to 0.5
- tensor_weight: float32 [128, 64], replicated, may hold values from -0.5 to 0.5
- first_gate: float32 [128, 64], replicated, may hold values from -0.5 to 0.5
- mix_weight: float32 [3, 64, 64], replicated, may hold values from -0.75 to 0.75
- first_latent: float32 [320, 128], replicated, may hold values from -0.3125 to 0.3125
- second_gate: float32 [128, 64], replicated, may hold values from -0.5 to 0.5
- second_latent: float32 [320, 128], replicated, may hold values from -0.3125 to 0.3125
- readout_weight: float32 [128, 128], replicated, may hold values from -0.5 to 0.5
- readout_vector: float32 [128], replicated, may hold values from -0.5 to 0.5
- self_weight: float32 [128], replicated, may hold values from -0.5 to 0.5
Outputs:
- forces: float32 [3, 64, 4, 128], P(None, 'gx', 'gy')
- atom_energy: float32 [64, 4, 128], P('gx', 'gy')
Inputs may be any that keep to these rules, and one draw needn't show every extreme that they name: `atom_count`: live atoms are the first slots of a domain; some domain is full. Edge slots from edge_count on are padding; some domain is full. A live edge's center is a live atom, and centers never fall along the live edges. `neighbours`: a live edge's neighbour is a live atom of the domain or a ghost slot. `send_across`: each list names distinct live atoms of the sending domain. `send_along`: each list names distinct live atoms of the sending domain. `send_corner`: each list names distinct live atoms of the sending domain.
All inputs are finite; a program needn't handle non-finite values.
Results may differ from a plain program's by a relative error of at most 0.00015.
Values sent between devices are 32-bit elements; how exact they have to be, the bound alone decides.
A program may use at most 64 MiB of HBM per device.

v0:
```python
import functools
import math

import jax
import jax.numpy as jnp
from jax import lax
from jax.experimental import pallas as pl
from jax.experimental.pallas import tpu as pltpu
from jax.sharding import PartitionSpec as P

f32 = jnp.float32
bf16 = jnp.bfloat16

ATOMS = 128
EDGES = 512
CH = 64
LAT = 128
BASIS = 8
WIDTH = 2.5 / (BASIS - 1)
ROOT3 = math.sqrt(3.0)
DEGREE = (0, 1, 1, 1, 2, 2, 2, 2, 2)
STEPS = ((1, 0), (-1, 0), (0, 1), (0, -1), (1, 1), (1, -1), (-1, 1), (-1, -1))
FIRST_LANE = (0, 64, 0, 16, 32, 36, 40, 44)
LANES = (64, 64, 16, 16, 4, 4, 4, 4)
PACK_ONE = ((2, 72), (2, 72), (6, 24), (6, 24), (18, 8), (18, 8), (18, 8), (18, 8))
PACK_TWO = ((2, 288), (2, 288), (8, 72), (8, 72), (24, 24), (24, 24), (24, 24), (24, 24))


def split(value):
    high = value.astype(bf16)
    return high, (value - high.astype(f32)).astype(bf16)


def mm(left, right):
    return jnp.dot(left, right, preferred_element_type=f32)


def side_by_side(value):
    return jnp.concatenate(split(value), axis=1)


def stacked(value):
    return jnp.concatenate(split(value), axis=0)


def weight_form(weight):
    high, low = split(weight)
    top = jnp.concatenate([high, high], axis=1)
    bottom = jnp.concatenate([low, jnp.zeros_like(low)], axis=1)
    return jnp.concatenate([top, bottom], axis=0)


def dense(form, stack):
    both = mm(form, stack)
    rows = both.shape[0] // 2
    return both[:rows] + both[rows:]


def iota(shape, axis):
    return lax.broadcasted_iota(jnp.int32, shape, axis)


def hot(mask):
    return jnp.where(mask, 1.0, 0.0).astype(bf16)


def rolled(value, shift):
    shift = shift % 128
    return value if shift == 0 else pltpu.roll(value, shift, 1)


def sigmoid_parts(value):
    gate = 1.0 / (1.0 + jnp.exp(-value))
    act = value * gate
    return act, gate + act * (1.0 - gate)


def body(
    grid,
    pos_ref, feat_ref, atom_count_ref, edge_count_ref, centre_ref, neigh_ref,
    across_ref, along_ref, corner_ref, radial_ref, pair_ref, tensor_ref, gate1_ref,
    mix_ref, latent1_ref, gate2_ref, latent2_ref, readout_ref, vector_ref, self_ref,
    force_ref, energy_ref,
    *scratch,
):
    scratch = list(scratch)

    def take(count):
        taken = scratch[:count]
        del scratch[:count]
        return taken

    out1, in1, out2, in2, out3, in3, in4 = (take(8) for _ in range(7))
    out4 = take(2)
    (
        hcn, hcnt, sel, selt, table1, table2, geo, lat, grads, big,
        g1, t1, joint, wide, mixed, pile, acc, env_own,
        pair_t, first_form, first_back, gate2_form, gate2_back, mix_form, mix_back, latent1_form,
        latent1_back, latent2_form, latent2_back, readout_form, readout_back, vector_col,
        radial_form, radial_back, gate_pair,
    ) = take(35)
    send_sem, recv_sem = take(2)

    def drow(m):
        return m * 8

    size_x, size_y = grid
    ix, iy = lax.axis_index("gx"), lax.axis_index("gy")

    def device(step, sign):
        dx, dy = step
        return (
            lax.rem(ix + (sign * dx + size_x), size_x),
            lax.rem(iy + (sign * dy + size_y), size_y),
        )

    still = lax.div(ix, size_x)

    def lat_rows(first):
        return lat[pl.ds(pl.multiple_of(still * 8, 8) + first, 128)]

    barrier = pltpu.get_barrier_semaphore()
    for step in STEPS:
        pl.semaphore_signal(
            barrier, inc=1, device_id=device(step, 1), device_id_type=pl.DeviceIdType.MESH
        )

    def copy(phase, k, source, target, sign):
        return pltpu.make_async_remote_copy(
            src_ref=source,
            dst_ref=target,
            send_sem=send_sem.at[phase, k],
            recv_sem=recv_sem.at[phase, k],
            device_id=device(STEPS[k], sign),
            device_id_type=pl.DeviceIdType.MESH,
        )

    lane = iota((8, 128), 1)

    def pack(plan, k, table, target):
        groups, rows = plan[k]
        at = lane[:1]
        total = None
        for g in range(groups):
            piece = rolled(table[g * rows : (g + 1) * rows], LANES[k] * g - FIRST_LANE[k])
            total = piece if g == 0 else jnp.where(at >= LANES[k] * g, piece, total)
        target[...] = total

    def unpack_x(plan, ins):
        at = lane[:1]
        low, high = ins[0][...], ins[1][...]
        top = jnp.where(at < 64, low, rolled(high, 64))
        bottom = jnp.where(at < 64, rolled(low, 64), high)
        return jnp.concatenate([top, bottom], axis=0)

    def unpack_s(plan, ins):
        at = lane[:1]
        step = plan[4][1]
        pieces = []
        for b in range(plan[4][0]):
            value = None
            for k in range(2, 8):
                rows = plan[k][1]
                g, first = (b * step) // rows, (b * step) % rows
                piece = rolled(ins[k][first : first + step], FIRST_LANE[k] - LANES[k] * g)
                value = piece if k == 2 else jnp.where(at >= FIRST_LANE[k], piece, value)
            pieces.append(value)
        return jnp.concatenate(pieces, axis=0)

    across, along, corner = across_ref[0, 0], along_ref[0, 0], corner_ref[0, 0]
    list_x = jnp.concatenate([across[1:2], across[0:1]], axis=1)
    list_s = jnp.concatenate(
        [along[1:2], along[0:1], corner[3:4], corner[2:3], corner[1:2], corner[0:1],
         jnp.full((1, 80), -1, jnp.int32)],
        axis=1,
    )
    lists = jnp.concatenate([list_x, list_s], axis=1)
    chosen = hot(iota((128, 256), 0) == lists)
    sel[0:128] = chosen
    sel[128:256] = chosen

    sub8 = iota((8, 128), 0)
    features = feat_ref[0, 0]
    pos_own = jnp.where(
        sub8 == 0, pos_ref[0, 0],
        jnp.where(sub8 == 1, pos_ref[1, 0], jnp.where(sub8 == 2, pos_ref[2, 0], 0.0)),
    )
    pos_high = pos_own.astype(bf16).astype(f32)
    pos_mid = (pos_own - pos_high).astype(bf16).astype(f32)
    pos_low = pos_own - pos_high - pos_mid
    raw = side_by_side(jnp.concatenate([features, pos_own, pos_low], axis=0))
    sent = mm(raw, sel[...])
    sent = jnp.concatenate([sent[:128], sent[128:136] + sent[136:144], sent[136:144]], axis=0)
    for k in range(8):
        pack(PACK_ONE, k, sent[:, 0:128] if k < 2 else sent[:, 128:256], out1[k])

    pl.semaphore_wait(barrier, 8)
    first_copies = [copy(0, k, out1[k], in1[k], 1) for k in range(8)]
    for one in first_copies:
        one.start()

    centre_row, neigh_row = centre_ref[0], neigh_ref[0]
    hot_c = hot(iota((128, EDGES), 0) == centre_row)
    hot_n = [hot(iota((128, EDGES), 0) + 128 * t == neigh_row) for t in range(3)]
    for t, value in enumerate([hot_c] + hot_n):
        hcn[256 * t : 256 * t + 128] = value
        hcn[256 * t + 128 : 256 * t + 256] = value
    centre_col = jnp.transpose(jnp.broadcast_to(centre_row.astype(f32), (128, EDGES)))
    neigh_col = jnp.transpose(jnp.broadcast_to(neigh_row.astype(f32), (128, EDGES)))
    lane_f = iota((1, 128), 1).astype(f32)
    hot_ct = hot(centre_col == lane_f)
    hot_nt = [hot(neigh_col == lane_f + 128.0 * t) for t in range(3)]
    for t, value in enumerate([hot_ct] + hot_nt):
        hcnt[0:EDGES, 128 * t : 128 * t + 128] = value
        hcnt[EDGES : 2 * EDGES, 128 * t : 128 * t + 128] = value
    selt_f = jnp.transpose(chosen.astype(f32)).astype(bf16)
    for t in range(2):
        selt[256 * t : 256 * t + 128] = selt_f[128 * t : 128 * t + 128]
        selt[256 * t + 128 : 256 * t + 256] = selt_f[128 * t : 128 * t + 128]

    def forward_form(weight):
        return weight_form(jnp.transpose(weight))

    def pair_form(first):
        both = jnp.transpose(first)
        high, low = split(both)
        low = jnp.where(iota((1, 128), 1) < 64, low.astype(f32), 0.0).astype(bf16)
        return jnp.concatenate([high, low], axis=0)

    pair_t[...] = forward_form(pair_ref[1])
    own_raw = stacked(features)
    table1[:, 0:256] = side_by_side(dense(forward_form(pair_ref[0]), own_raw))
    table1[:, 256:512] = side_by_side(dense(pair_t[...], own_raw))
    self_rows = jnp.broadcast_to(self_ref[...].reshape(1, LAT), (16, LAT))
    self_row = dense(weight_form(self_rows), own_raw)[0:1]
    zeros64 = jnp.zeros((64, LAT), f32)
    first_t = jnp.concatenate([jnp.transpose(tensor_ref[...]), jnp.transpose(gate1_ref[...])], axis=0)
    first_form[...] = weight_form(first_t)
    first_back[...] = forward_form(first_t)
    gate2_t = jnp.transpose(gate2_ref[...])
    gate2_form[...] = weight_form(gate2_t)
    gate2_back[...] = forward_form(jnp.concatenate([gate2_t, zeros64], axis=0))
    for d in range(3):
        weight = mix_ref[d]
        turned = jnp.transpose(weight)
        mix_form[d] = pair_form(jnp.concatenate([weight, weight], axis=0))
        mix_back[d] = pair_form(jnp.concatenate([turned, turned], axis=0))
    latent1_form[...] = forward_form(jnp.concatenate([latent1_ref[...], zeros64], axis=0))
    latent1_back[...] = weight_form(latent1_ref[...])
    latent2_form[...] = forward_form(jnp.concatenate([latent2_ref[...], zeros64], axis=0))
    latent2_back[...] = weight_form(latent2_ref[...])
    readout_form[...] = forward_form(readout_ref[...])
    readout_back[...] = weight_form(readout_ref[...])
    vector_col[...] = jnp.transpose(jnp.broadcast_to(vector_ref[...].reshape(1, LAT), (128, LAT)))
    radial_full = jnp.concatenate([radial_ref[...], jnp.zeros((120, LAT), f32)], axis=0)
    radial_form[...] = forward_form(radial_full)
    radial_back[...] = weight_form(radial_full[:16])

    for one in first_copies:
        one.wait()
    table_x, table_s = unpack_x(PACK_ONE, in1), unpack_s(PACK_ONE, in1)
    ghost_raw = jnp.concatenate([table_x[:128], table_s[:128]], axis=1)
    ghost_proj = dense(pair_t[...], stacked(ghost_raw))
    table1[:, 512:768] = side_by_side(ghost_proj[:, 0:128])
    table1[:, 768:1024] = side_by_side(ghost_proj[:, 128:256])

    def offsets(rows):
        total = jnp.zeros((8, 128), f32)
        for k in rows:
            dx, dy = STEPS[k]
            inside = (lane >= FIRST_LANE[k]) & (lane < FIRST_LANE[k] + LANES[k])
            total = jnp.where(inside & (sub8 == 0), -1.0 * dx, total)
            total = jnp.where(inside & (sub8 == 1), -1.0 * dy, total)
        return total

    positions = jnp.concatenate(
        [pos_own, table_x[128:136] + offsets((0, 1)), table_s[128:136] + offsets(range(2, 8))], axis=1
    )
    p_high = positions.astype(bf16).astype(f32)
    p_mid = (positions - p_high).astype(bf16).astype(f32)
    p_low = positions - p_high - p_mid
    parts = jnp.concatenate([p_high, p_mid, p_low, jnp.zeros_like(p_low)], axis=0).astype(bf16)
    moved = mm(parts[:, 0:128], hcn[256:384] - hcn[0:128])
    moved += mm(parts[:, 128:256], hcn[512:640]) + mm(parts[:, 256:384], hcn[768:896])
    moved = moved[0:8] + moved[8:16] + moved[16:24]

    length = jnp.sqrt(jnp.sum(moved * moved, axis=0, keepdims=True) + 0.25)
    inverse = 1.0 / length
    unit = moved * inverse
    ux, uy, uz = unit[0:1], unit[1:2], unit[2:3]
    live = (iota((1, EDGES), 1) < edge_count_ref[0, 0]).astype(f32)
    falloff = 1.0 / (1.0 + 0.25 * length * length)
    envelope = live * falloff
    square = ux * ux + uy * uy + uz * uz
    shapes = [
        jnp.ones_like(ux), ux, uy, uz, ROOT3 * ux * uy, ROOT3 * uy * uz,
        0.5 * (3.0 * uz * uz - square), ROOT3 * ux * uz, 0.5 * ROOT3 * (ux * ux - uy * uy),
    ]
    for m in range(9):
        geo[drow(m) : drow(m) + 8] = jnp.broadcast_to(shapes[m], (8, EDGES))
    geo[72:80] = jnp.broadcast_to(envelope, (8, EDGES))

    mid_points = 0.5 + WIDTH * iota((BASIS, EDGES), 0).astype(f32)
    scaled = (length - mid_points) / WIDTH
    basis = jnp.exp(-(scaled * scaled))
    basis_full = jnp.concatenate([basis, jnp.zeros((120, EDGES), f32)], axis=0)
    before0 = dense(radial_form[...], stacked(basis_full)) + mm(table1[...], hcn[...])
    latent0, slope0 = sigmoid_parts(before0)
    lat[0:128] = slope0
    lat[128:256] = latent0
    high0, low0 = split(latent0)
    pile[0:128] = high0
    pile[384:512] = low0
    gains = dense(first_form[...], jnp.concatenate([high0, low0], axis=0))
    grads[0:128] = gains

    def lanes_at(t):
        return pl.ds(pl.multiple_of(t * 128, 128), 128)

    def shape_at(m, at):
        return geo[m * 8 : m * 8 + 1, at]

    def write_wide(row, t, value):
        high, low = split(value)
        wide[row : row + 16, lanes_at(t)] = high
        wide[row : row + 16, lanes_at(t + 4)] = low

    def spread(source, row0):
        def tile(t, carry):
            at = lanes_at(t)
            weight = 0.5 * geo[72:73, at]
            for c in range(4):
                gate = source[row0 + 16 * c : row0 + 16 * c + 16, at] * weight
                for m in range(9):
                    value = gate if m == 0 else gate * shape_at(m, at)
                    write_wide(64 * m + 16 * c, t, value)
            return carry

        lax.fori_loop(0, 4, tile, 0)

    spread(grads, 64)
    environment = mm(wide[...], hcnt[:, 0:128])
    env_pair = side_by_side(environment)
    table2[:, 256:512] = env_pair
    sent = mm(env_pair, sel[...])
    second_copies = [copy(1, k, out2[k], in2[k], 1) for k in range(8)]
    for k in range(8):
        pack(PACK_TWO, k, sent[:, 0:128] if k < 2 else sent[:, 128:256], out2[k])
        second_copies[k].start()

    g1[...] = mm(env_pair, hcn[0:256])

    def couple(t, carry):
        at = lanes_at(t)
        y = [None] + [shape_at(m, at) for m in range(1, 9)]
        for c in range(4):
            gain = grads[16 * c : 16 * c + 16, at]
            g = [g1[64 * m + 16 * c : 64 * m + 16 * c + 16, at] for m in range(9)]
            inner = [g[0] + g[0]] + [y[m] * g[0] + g[m] for m in range(1, 9)]
            inner[1] = inner[1] + (y[2] * g[3] - y[3] * g[2])
            inner[2] = inner[2] + (y[3] * g[1] - y[1] * g[3])
            inner[3] = inner[3] + (y[1] * g[2] - y[2] * g[1])
            for m in range(9):
                high, low = split(gain * inner[m])
                mixed[m, 16 * c : 16 * c + 16, at] = high
                mixed[m, 64 + 16 * c : 80 + 16 * c, at] = low
            sums = [
                g[0],
                y[1] * g[1] + y[2] * g[2] + y[3] * g[3],
                y[4] * g[4] + y[5] * g[5] + y[6] * g[6] + y[7] * g[7] + y[8] * g[8],
            ]
            for d in range(3):
                high, low = split(gain * sums[d])
                row = 128 + 64 * d + 16 * c
                pile[row : row + 16, at] = high
                pile[384 + row : 400 + row, at] = low
        return carry

    lax.fori_loop(0, 4, couple, 0)
    nothing = jnp.zeros((64, EDGES), bf16)
    pile[320:384] = nothing
    pile[704:768] = nothing
    act1, slope1 = sigmoid_parts(dense(latent1_form[...], pile[...]))
    lat[256:384] = slope1
    latent1 = lat_rows(128) + act1
    lat[384:512] = latent1
    high1, low1 = split(latent1)
    pile[0:128] = high1
    pile[384:512] = low1
    grads[128:192] = dense(gate2_form[...], jnp.concatenate([high1, low1], axis=0))
    spread(grads, 128)
    table2[:, 0:256] = side_by_side(mm(wide[...], hcnt[:, 0:128]))
    joint[...] = mm(table2[:, 0:512], hcn[0:512])
    for m in range(9):
        t1[64 * m : 64 * m + 64] = dense(mix_form[DEGREE[m]], mixed[m])

    for k in range(2):
        second_copies[k].wait()
    table2[:, 512:768] = side_by_side(unpack_x(PACK_TWO, in2))
    for k in range(2, 8):
        second_copies[k].wait()
    table2[:, 768:1024] = side_by_side(unpack_s(PACK_TWO, in2))
    joint[...] += mm(table2[:, 512:1024], hcn[512:1024])

    def contract(t, carry):
        at = lanes_at(t)
        for c in range(4):
            sums = [None, None, None]
            for m in range(9):
                row = 64 * m + 16 * c
                term = t1[row : row + 16, at] * joint[row : row + 16, at]
                d = DEGREE[m]
                sums[d] = term if sums[d] is None else sums[d] + term
            for d in range(3):
                high, low = split(sums[d])
                row = 128 + 64 * d + 16 * c
                pile[row : row + 16, at] = high
                pile[384 + row : 400 + row, at] = low
        return carry

    lax.fori_loop(0, 4, contract, 0)
    act2, slope2 = sigmoid_parts(dense(latent2_form[...], pile[...]))
    latent2 = lat_rows(384) + act2
    hidden, slope_h = sigmoid_parts(dense(readout_form[...], stacked(latent2)))
    vector_wide = jnp.concatenate([vector_col[...]] * 4, axis=1)
    energy_raw = jnp.sum(vector_wide * hidden, axis=0, keepdims=True)
    edge_energy = envelope * energy_raw

    d_hidden = vector_wide * envelope * slope_h
    d_latent2 = dense(readout_back[...], stacked(d_hidden))
    d_pile = dense(latent2_back[...], stacked(d_latent2 * slope2))
    lat[512:640] = d_latent2 + d_pile[0:128]
    grads[192:384] = d_pile[128:320]

    def joint_back(t, carry):
        at = lanes_at(t)
        for c in range(4):
            d_sum = [grads[192 + 64 * d + 16 * c : 208 + 64 * d + 16 * c, at] for d in range(3)]
            for m in range(9):
                row = 64 * m + 16 * c
                write_wide(row, t, t1[row : row + 16, at] * d_sum[DEGREE[m]])
        return carry

    lax.fori_loop(0, 4, joint_back, 0)
    back = mm(wide[...], hcnt[:, 256:512])
    third_copies = [copy(2, k, out3[k], in3[k], -1) for k in range(8)]
    for k in range(8):
        pack(PACK_TWO, k, back[:, 0:128] if k < 2 else back[:, 128:256], out3[k])
        third_copies[k].start()

    back = mm(wide[...], hcnt[:, 0:256])
    env_own[...] = back[:, 128:256]
    big[...] = mm(side_by_side(back[:, 0:128]), hcn[0:256])

    def mix_grads(t, carry):
        at = lanes_at(t)
        for c in range(4):
            d_sum = [grads[192 + 64 * d + 16 * c : 208 + 64 * d + 16 * c, at] for d in range(3)]
            for m in range(9):
                row = 64 * m + 16 * c
                high, low = split(joint[row : row + 16, at] * d_sum[DEGREE[m]])
                mixed[m, 16 * c : 16 * c + 16, at] = high
                mixed[m, 64 + 16 * c : 80 + 16 * c, at] = low
        return carry

    lax.fori_loop(0, 4, mix_grads, 0)
    for m in range(9):
        joint[64 * m : 64 * m + 64] = dense(mix_back[DEGREE[m]], mixed[m])

    def halves(value):
        return value[0:8] + value[8:16]

    def spread_back(source, row0, target0, fresh):
        def tile(t, carry):
            at = lanes_at(t)
            half = 0.5 * geo[72:73, at]
            d_shape = [None] * 9
            d_env = None
            for c in range(4):
                gate = source[row0 + 16 * c : row0 + 16 * c + 16, at]
                weight = gate * half
                total = None
                for m in range(9):
                    row = 64 * m + 16 * c
                    value = big[row : row + 16, at]
                    if m:
                        term = halves(value * weight)
                        d_shape[m] = term if c == 0 else d_shape[m] + term
                        value = value * shape_at(m, at)
                    total = value if m == 0 else total + value
                grads[target0 + 16 * c : target0 + 16 * c + 16, at] = total * half
                term = halves(total * gate)
                d_env = term if c == 0 else d_env + term
            d_env = 0.5 * d_env
            for m in range(1, 9):
                if fresh:
                    acc[drow(m) : drow(m) + 8, at] = d_shape[m]
                else:
                    acc[drow(m) : drow(m) + 8, at] += d_shape[m]
            if fresh:
                acc[0:8, at] = d_env
            else:
                acc[0:8, at] += d_env
            return carry

        lax.fori_loop(0, 4, tile, 0)

    spread_back(grads, 128, 384, True)
    gate_high, gate_low = split(grads[384:448])
    gate_pair[0:64] = gate_high
    gate_pair[64:128] = nothing
    gate_pair[128:192] = gate_low
    gate_pair[192:256] = nothing
    d_latent1 = lat_rows(512) + dense(gate2_back[...], gate_pair[...])
    d_pile = dense(latent1_back[...], stacked(d_latent1 * lat_rows(256)))
    lat[640:768] = d_latent1 + d_pile[0:128]
    grads[192:384] = d_pile[128:320]

    def couple_back(t, carry):
        at = lanes_at(t)
        y = [None] + [shape_at(m, at) for m in range(1, 9)]
        d_shape = [None] * 9
        for c in range(4):
            gain = grads[16 * c : 16 * c + 16, at]
            g = [g1[64 * m + 16 * c : 64 * m + 16 * c + 16, at] for m in range(9)]
            u = [joint[64 * m + 16 * c : 64 * m + 16 * c + 16, at] for m in range(9)]
            s = [grads[192 + 64 * d + 16 * c : 208 + 64 * d + 16 * c, at] for d in range(3)]
            inner = [g[0] + g[0]] + [y[m] * g[0] + g[m] for m in range(1, 9)]
            inner[1] = inner[1] + (y[2] * g[3] - y[3] * g[2])
            inner[2] = inner[2] + (y[3] * g[1] - y[1] * g[3])
            inner[3] = inner[3] + (y[1] * g[2] - y[2] * g[1])
            d_gain = s[0] * g[0]
            for m in range(9):
                d_gain = d_gain + u[m] * inner[m]
            d_gain = d_gain + s[1] * (y[1] * g[1] + y[2] * g[2] + y[3] * g[3])
            d_gain = d_gain + s[2] * (
                y[4] * g[4] + y[5] * g[5] + y[6] * g[6] + y[7] * g[7] + y[8] * g[8]
            )
            grads[448 + 16 * c : 464 + 16 * c, at] = d_gain
            k = [gain * value for value in u]
            q = [gain * value for value in s]
            d_g = [k[0] + k[0] + q[0]] + [k[m] + q[DEGREE[m]] * y[m] for m in range(1, 9)]
            for m in range(1, 9):
                d_g[0] = d_g[0] + k[m] * y[m]
            d_g[1] = d_g[1] + (k[2] * y[3] - k[3] * y[2])
            d_g[2] = d_g[2] + (k[3] * y[1] - k[1] * y[3])
            d_g[3] = d_g[3] + (k[1] * y[2] - k[2] * y[1])
            d_y = [None] + [k[m] * g[0] + q[DEGREE[m]] * g[m] for m in range(1, 9)]
            d_y[1] = d_y[1] + (k[3] * g[2] - k[2] * g[3])
            d_y[2] = d_y[2] + (k[1] * g[3] - k[3] * g[1])
            d_y[3] = d_y[3] + (k[2] * g[1] - k[1] * g[2])
            for m in range(1, 9):
                term = halves(d_y[m])
                d_shape[m] = term if c == 0 else d_shape[m] + term
            for m in range(9):
                write_wide(64 * m + 16 * c, t, d_g[m])
        for m in range(1, 9):
            acc[drow(m) : drow(m) + 8, at] += d_shape[m]
        return carry

    lax.fori_loop(0, 4, couple_back, 0)
    env_own[...] += mm(wide[...], hcnt[:, 0:128])

    for one in third_copies:
        one.wait()
    ghosts = jnp.concatenate(
        [side_by_side(unpack_x(PACK_TWO, in3)), side_by_side(unpack_s(PACK_TWO, in3))], axis=1
    )
    d_environment = env_own[...] + mm(ghosts, selt[...])
    big[...] = mm(side_by_side(d_environment), hcn[0:256])
    spread_back(grads, 64, 512, False)
    d_latent0 = lat_rows(640) + dense(first_back[...], stacked(grads[448:576]))
    d_basis = dense(radial_back[...], stacked(d_latent0 * lat_rows(0)))[:8]
    d_length = jnp.sum(d_basis * basis * scaled, axis=0, keepdims=True) * (-2.0 / WIDTH)
    d_env = jnp.sum(acc[0:8], axis=0, keepdims=True) + energy_raw
    d_length = d_length - 0.5 * length * envelope * falloff * d_env
    d_y = [None] + [jnp.sum(acc[drow(m) : drow(m) + 8], axis=0, keepdims=True) for m in range(1, 9)]
    d_ux = d_y[1] + ROOT3 * (uy * d_y[4] + uz * d_y[7] + ux * d_y[8]) - ux * d_y[6]
    d_uy = d_y[2] + ROOT3 * (ux * d_y[4] + uz * d_y[5] - uy * d_y[8]) - uy * d_y[6]
    d_uz = d_y[3] + ROOT3 * (uy * d_y[5] + ux * d_y[7]) + 2.0 * (uz * d_y[6])
    d_length = d_length - (d_ux * ux + d_uy * uy + d_uz * uz) * inverse
    sub_e = iota((8, EDGES), 0)
    d_unit = jnp.where(sub_e == 0, d_ux, jnp.where(sub_e == 1, d_uy, jnp.where(sub_e == 2, d_uz, 0.0)))
    d_moved = d_unit * inverse + d_length * unit

    def folded(value):
        high = value.astype(bf16).astype(f32)
        return jnp.concatenate([high, value - high], axis=0).astype(bf16)

    d_parts = folded(d_moved)
    d_table = halves(mm(d_parts, hcnt[0:EDGES, 128:512]))
    d_centre = halves(mm(d_parts, hcnt[0:EDGES, 0:128]))
    out4[0][...] = d_table[:, 128:256]
    out4[1][...] = d_table[:, 256:384]
    last_copies = [copy(3, k, out4[0] if k < 2 else out4[1], in4[k], -1) for k in range(8)]
    for one in last_copies:
        one.start()
    d_own = d_table[:, 0:128] - d_centre

    per_atom = halves(mm(folded(jnp.broadcast_to(edge_energy, (8, EDGES))), hcnt[0:EDGES, 0:128]))[0:1]
    alive = (iota((1, ATOMS), 1) < atom_count_ref[0, 0]).astype(f32)
    energy_ref[0] = alive * (per_atom + self_row)

    for one in last_copies:
        one.wait()
    grad_x = jnp.where(lane < 64, in4[0][...], in4[1][...])
    grad_s = in4[2][...]
    for k in range(3, 8):
        grad_s = jnp.where(lane >= FIRST_LANE[k], in4[k][...], grad_s)
    returned = mm(folded(grad_x), selt[0:128]) + mm(folded(grad_s), selt[256:384])
    total = d_own + halves(returned)
    for axis in range(3):
        force_ref[axis, 0] = -total[axis : axis + 1]


def per_device(grid, *args):
    vmem = pl.BlockSpec(memory_space=pltpu.VMEM)
    smem = pl.BlockSpec(memory_space=pltpu.SMEM)
    specs = [vmem] * len(args)
    specs[2] = specs[3] = smem
    packs = [
        [pltpu.VMEM((plan[k][1], 128), f32) for k in range(8)] for plan in (PACK_ONE, PACK_TWO)
    ]
    small = [pltpu.VMEM((8, 128), f32)]
    scratch = packs[0] * 2 + packs[1] * 4 + small * 8 + small * 2
    scratch += [
        pltpu.VMEM((1024, EDGES), bf16),
        pltpu.VMEM((2 * EDGES, 512), bf16),
        pltpu.VMEM((256, 256), bf16),
        pltpu.VMEM((512, 128), bf16),
        pltpu.VMEM((128, 1024), bf16),
        pltpu.VMEM((576, 1024), bf16),
        pltpu.VMEM((80, EDGES), f32),
        pltpu.VMEM((768, EDGES), f32),
        pltpu.VMEM((576, EDGES), f32),
        pltpu.VMEM((576, EDGES), f32),
        pltpu.VMEM((576, EDGES), f32),
        pltpu.VMEM((576, EDGES), f32),
        pltpu.VMEM((576, EDGES), f32),
        pltpu.VMEM((576, 2 * EDGES), bf16),
        pltpu.VMEM((9, 128, EDGES), bf16),
        pltpu.VMEM((768, EDGES), bf16),
        pltpu.VMEM((72, EDGES), f32),
        pltpu.VMEM((576, 128), f32),
        *(
            pltpu.VMEM(shape, bf16)
            for shape in (
                (256, 256), (256, 256), (256, 256), (128, 256), (256, 256), (3, 128, 128),
                (3, 128, 128), (256, 768), (640, 256), (256, 768), (640, 256), (256, 256), (256, 256),
            )
        ),
        pltpu.VMEM((128, 128), f32),
        pltpu.VMEM((256, 256), bf16),
        pltpu.VMEM((32, 256), bf16),
        pltpu.VMEM((256, EDGES), bf16),
        pltpu.SemaphoreType.DMA((4, 8)),
        pltpu.SemaphoreType.DMA((4, 8)),
    ]
    return pl.pallas_call(
        functools.partial(body, grid),
        out_shape=(
            jax.ShapeDtypeStruct((3, 1, 1, ATOMS), f32),
            jax.ShapeDtypeStruct((1, 1, ATOMS), f32),
        ),
        in_specs=specs,
        out_specs=(vmem, vmem),
        scratch_shapes=scratch,
        compiler_params=pltpu.CompilerParams(
            collective_id=0, has_side_effects=True, vmem_limit_bytes=48 * 1024 * 1024
        ),
    )(*args)


def solution(mesh):
    grid = (mesh.shape["gx"], mesh.shape["gy"])
    edge = P("gx", "gy", None)
    lists = P("gx", "gy", None, None)
    return jax.shard_map(
        functools.partial(per_device, grid),
        mesh=mesh,
        in_specs=(P(None, "gx", "gy", None), lists, P("gx", "gy"), P("gx", "gy"), edge, edge)
        + (lists,) * 3
        + (P(),) * 11,
        out_specs=(P(None, "gx", "gy", None), edge),
        check_vma=False,
    )
```

profile of v0, /device:TPU:1, one launch (start us, length us, event | category | flops | bytes accessed | tf_op | source)
XLA Modules:
  0.0 65.0 jit_solution(7502604677561259021)
XLA Ops:
  0.6 0.0 copy-start
  2.0 0.0 copy-start.2
  2.0 0.9 %copy.22.tensor_ref = f32[128,64]{1,0:T(8,128)S(1)} copy(f32[128,64]{0,1:T(8,128)} %param.31) | data formatting | bytes 65536 | tf_op args[11]
  2.9 0.9 %copy.23.gate1_ref = f32[128,64]{1,0:T(8,128)S(1)} copy(f32[128,64]{0,1:T(8,128)} %param.32) | data formatting | bytes 65536 | tf_op args[12]
  3.7 0.0 copy-start.7
  3.7 0.0 copy-start.10
  3.8 0.9 %copy.24.gate2_ref = f32[128,64]{1,0:T(8,128)S(1)} copy(f32[128,64]{0,1:T(8,128)} %param.35) | data formatting | bytes 65536 | tf_op args[15]
  4.6 0.0 copy-done
  4.6 0.0 copy-done.2
  4.6 0.0 copy-done.7
  4.6 0.0 copy-done.10
  4.7 0.0 copy-start.1
  4.7 0.9 %copy-done.1 = f32[320,128]{1,0:T(8,128)S(1)} copy-done((f32[320,128]{1,0:T(8,128)S(1)}, f32[320,128]{1,0:T(8,128)}, u32[]{:S(2)}) %copy-start.1) | copy-done | bytes 163864
  5.6 0.0 copy-start.3
  5.6 0.9 %copy-done.3 = f32[3,64,64]{2,1,0:T(8,128)S(1)} copy-done((f32[3,64,64]{2,1,0:T(8,128)S(1)}, f32[3,64,64]{2,1,0:T(8,128)}, u32[]{:S(2)}) %copy-start.3) | copy-done | bytes 49176
  6.5 0.0 copy-start.4
  6.5 0.8 %copy-done.4 = f32[1,1,128,128]{3,2,1,0:T(8,128)S(1)} copy-done((f32[1,1,128,128]{3,2,1,0:T(8,128)S(1)}, f32[1,1,128,128]{3,2,1,0:T(8,128)}, u32[]{:S(2)}) %copy-start.4) | copy-done | bytes 65560
  7.3 0.0 copy-start.5
  7.3 0.8 %copy-done.5 = f32[128,128]{1,0:T(8,128)S(1)} copy-done((f32[128,128]{1,0:T(8,128)S(1)}, f32[128,128]{1,0:T(8,128)}, u32[]{:S(2)}) %copy-start.5) | copy-done | bytes 65560
  8.1 0.0 copy-start.6
  8.2 0.7 %copy-done.6 = f32[8,128]{1,0:T(8,128)S(1)} copy-done((f32[8,128]{1,0:T(8,128)S(1)}, f32[8,128]{1,0:T(8,128)}, u32[]{:S(2)}) %copy-start.6) | copy-done | bytes 4120
  8.8 0.0 copy-start.8
  8.8 0.7 %copy-done.8 = s32[1,1,512]{2,1,0:T(1,128)S(1)} copy-done((s32[1,1,512]{2,1,0:T(1,128)S(1)}, s32[1,1,512]{2,1,0:T(1,128)}, u32[]{:S(2)}) %copy-start.8) | copy-done | bytes 2072
  9.5 0.0 copy-start.9
  9.5 0.7 %copy-done.9 = s32[1,1,4,4]{3,2,1,0:T(4,128)S(1)} copy-done((s32[1,1,4,4]{3,2,1,0:T(4,128)S(1)}, s32[1,1,4,4]{3,2,1,0:T(4,128)}, u32[]{:S(2)}) %copy-start.9) | copy-done | bytes 88
  10.2 0.0 copy-start.11
  10.2 0.7 %copy-done.11 = s32[1,1,2,64]{3,2,1,0:T(2,128)S(1)} copy-done((s32[1,1,2,64]{3,2,1,0:T(2,128)S(1)}, s32[1,1,2,64]{3,2,1,0:T(2,128)}, u32[]{:S(2)}) %copy-start.11) | copy-done | bytes 536
  10.9 0.0 copy-start.12
  10.9 0.7 %copy-done.12 = s32[1,1,2,16]{3,2,1,0:T(2,128)S(1)} copy-done((s32[1,1,2,16]{3,2,1,0:T(2,128)S(1)}, s32[1,1,2,16]{3,2,1,0:T(2,128)}, u32[]{:S(2)}) %copy-start.12) | copy-done | bytes 152
  11.6 0.0 copy-start.13
  11.6 0.7 %copy-done.13 = f32[128]{0:T(128)S(1)} copy-done((f32[128]{0:T(128)S(1)}, f32[128]{0:T(128)}, u32[]{:S(2)}) %copy-start.13) | copy-done | bytes 536
  12.2 0.0 copy-start.14
  12.2 0.7 %copy-done.14 = f32[128]{0:T(128)S(1)} copy-done((f32[128]{0:T(128)S(1)}, f32[128]{0:T(128)}, u32[]{:S(2)}) %copy-start.14) | copy-done | bytes 536
  12.9 51.0 %shard_map.203 = (f32[3,1,1,128]{3,2,1,0:T(1,128)S(1)}, f32[1,1,128]{2,1,0:T(1,128)S(1)}) custom-call(f32[3,1,1,128]{3,2,1,0:T(1,128)S(1)} %copy-done.10, f32[1,1,128,128]{3,2,1,0:T(8,128)S(1)} %copy-done.4, s32[1,1]{1,0:T(1,128)S(6)} %copy.27.atom_count_ref, s32[1,1]{1,0:T(1,128)S(6)} %copy.28.edge_count_ref, s32[1,1,512]{2,1,0:T(1,128)S(1)} %copy-done.7, ...), custom_call_target="tpu_custom_call" | custom-call | tf_op jit(solution)/shard_map/pallas_call | solution.py:659
  63.9 0.6 copy.29
  64.5 0.5 copy.30
Async XLA Ops:
  0.6 4.0 %copy-start = (f32[320,128]{1,0:T(8,128)S(1)}, f32[320,128]{1,0:T(8,128)}, u32[]{:S(2)}) copy-start(f32[320,128]{1,0:T(8,128)} %latent1_ref.1) | copy-start | bytes 491524
  2.0 2.7 %copy-start.2 = (f32[2,128,128]{2,1,0:T(8,128)S(1)}, f32[2,128,128]{2,1,0:T(8,128)}, u32[]{:S(2)}) copy-start(f32[2,128,128]{2,1,0:T(8,128)} %pair_ref.1) | copy-start | bytes 393220
  3.7 0.9 %copy-start.7 = (s32[1,1,512]{2,1,0:T(1,128)S(1)}, s32[1,1,512]{2,1,0:T(1,128)}, u32[]{:S(2)}) copy-start(s32[1,1,512]{2,1,0:T(1,128)} %centre_ref.1) | copy-start | bytes 6148
  3.7 0.9 %copy-start.10 = (f32[3,1,1,128]{3,2,1,0:T(1,128)S(1)}, f32[3,1,1,128]{3,2,1,0:T(1,128)}, u32[]{:S(2)}) copy-start(f32[3,1,1,128]{3,2,1,0:T(1,128)} %pos_ref.1) | copy-start | bytes 4612
  4.7 0.9 %copy-start.1 = (f32[320,128]{1,0:T(8,128)S(1)}, f32[320,128]{1,0:T(8,128)}, u32[]{:S(2)}) copy-start(f32[320,128]{1,0:T(8,128)} %latent2_ref.1) | copy-start | bytes 491524
  5.6 0.9 %copy-start.3 = (f32[3,64,64]{2,1,0:T(8,128)S(1)}, f32[3,64,64]{2,1,0:T(8,128)}, u32[]{:S(2)}) copy-start(f32[3,64,64]{2,1,0:T(8,128)} %mix_ref.1) | copy-start | bytes 147460
  6.5 0.8 %copy-start.4 = (f32[1,1,128,128]{3,2,1,0:T(8,128)S(1)}, f32[1,1,128,128]{3,2,1,0:T(8,128)}, u32[]{:S(2)}) copy-start(f32[1,1,128,128]{3,2,1,0:T(8,128)} %feat_ref.1) | copy-start | bytes 196612
  7.3 0.8 %copy-start.5 = (f32[128,128]{1,0:T(8,128)S(1)}, f32[128,128]{1,0:T(8,128)}, u32[]{:S(2)}) copy-start(f32[128,128]{1,0:T(8,128)} %readout_ref.1) | copy-start | bytes 196612
  8.1 0.7 %copy-start.6 = (f32[8,128]{1,0:T(8,128)S(1)}, f32[8,128]{1,0:T(8,128)}, u32[]{:S(2)}) copy-start(f32[8,128]{1,0:T(8,128)} %radial_ref.1) | copy-start | bytes 12292
  8.8 0.7 %copy-start.8 = (s32[1,1,512]{2,1,0:T(1,128)S(1)}, s32[1,1,512]{2,1,0:T(1,128)}, u32[]{:S(2)}) copy-start(s32[1,1,512]{2,1,0:T(1,128)} %neigh_ref.1) | copy-start | bytes 6148
  9.5 0.7 %copy-start.9 = (s32[1,1,4,4]{3,2,1,0:T(4,128)S(1)}, s32[1,1,4,4]{3,2,1,0:T(4,128)}, u32[]{:S(2)}) copy-start(s32[1,1,4,4]{3,2,1,0:T(4,128)} %corner_ref.1) | copy-start | bytes 196
  10.2 0.7 %copy-start.11 = (s32[1,1,2,64]{3,2,1,0:T(2,128)S(1)}, s32[1,1,2,64]{3,2,1,0:T(2,128)}, u32[]{:S(2)}) copy-start(s32[1,1,2,64]{3,2,1,0:T(2,128)} %across_ref.1) | copy-start | bytes 1540
  10.9 0.7 %copy-start.12 = (s32[1,1,2,16]{3,2,1,0:T(2,128)S(1)}, s32[1,1,2,16]{3,2,1,0:T(2,128)}, u32[]{:S(2)}) copy-start(s32[1,1,2,16]{3,2,1,0:T(2,128)} %along_ref.1) | copy-start | bytes 388
  11.6 0.7 %copy-start.13 = (f32[128]{0:T(128)S(1)}, f32[128]{0:T(128)}, u32[]{:S(2)}) copy-start(f32[128]{0:T(128)} %vector_ref.1) | copy-start | bytes 1540
  12.2 0.7 %copy-start.14 = (f32[128]{0:T(128)S(1)}, f32[128]{0:T(128)}, u32[]{:S(2)}) copy-start(f32[128]{0:T(128)} %self_ref.1) | copy-start | bytes 1540
where the time goes:
time: 65.5 us; the launch traced here: 65 us
  Pallas kernels  51 us (78%)
  local copies, waits for them, and re-layouts  11.9 us (18%)
  between operations  2.07 us (3%)
    pallas_call x1, Pallas kernels, per_device(): pl.pallas_call(functools.partial(body, grid), out_shape=(jax.ShapeDtypeSt...  51 us
    unnamed x35, local copies, waits for them, and re-layouts  11.9 us

commit v1 on v0

--- a/solution.py
+++ b/solution.py
@@ -26,6 +26,9 @@
 PACK_TWO = ((2, 288), (2, 288), (8, 72), (8, 72), (24, 24), (24, 24), (24, 24), (24, 24))
 
 
+FETCH_FIRST = (0, 1, 4, 5, 6)
+
+
 def split(value):
     high = value.astype(bf16)
     return high, (value - high.astype(f32)).astype(bf16)
@@ -77,13 +80,26 @@
 
 def body(
     grid,
-    pos_ref, feat_ref, atom_count_ref, edge_count_ref, centre_ref, neigh_ref,
-    across_ref, along_ref, corner_ref, radial_ref, pair_ref, tensor_ref, gate1_ref,
-    mix_ref, latent1_ref, gate2_ref, latent2_ref, readout_ref, vector_ref, self_ref,
-    force_ref, energy_ref,
-    *scratch,
+    atom_count_ref, edge_count_ref, *refs,
 ):
+    sources, (force_ref, energy_ref), scratch = refs[:18], refs[18:20], refs[20:]
     scratch = list(scratch)
+
+    (
+        pos_ref, feat_ref, centre_ref, neigh_ref, across_ref, along_ref, corner_ref, radial_ref,
+        pair_ref, tensor_ref, gate1_ref, mix_ref, latent1_ref, gate2_ref, latent2_ref, readout_ref,
+        vector_ref, self_ref, fetch_sem,
+    ) = scratch[:19]
+    fetches = [
+        pltpu.make_async_copy(source, target, fetch_sem.at[i])
+        for i, (source, target) in enumerate(zip(sources, scratch[:18]))
+    ]
+    for i in FETCH_FIRST:
+        fetches[i].start()
+    for i in range(18):
+        if i not in FETCH_FIRST:
+            fetches[i].start()
+    del scratch[:19]
 
     def take(count):
         taken = scratch[:count]
@@ -166,6 +182,9 @@
                 value = piece if k == 2 else jnp.where(at >= FIRST_LANE[k], piece, value)
             pieces.append(value)
         return jnp.concatenate(pieces, axis=0)
+
+    for i in FETCH_FIRST:
+        fetches[i].wait()
 
     across, along, corner = across_ref[0, 0], along_ref[0, 0], corner_ref[0, 0]
     list_x = jnp.concatenate([across[1:2], across[0:1]], axis=1)
@@ -199,6 +218,8 @@
     for one in first_copies:
         one.start()
 
+    for i in (2, 3):
+        fetches[i].wait()
     centre_row, neigh_row = centre_ref[0], neigh_ref[0]
     hot_c = hot(iota((128, EDGES), 0) == centre_row)
     hot_n = [hot(iota((128, EDGES), 0) + 128 * t == neigh_row) for t in range(3)]
@@ -227,6 +248,8 @@
         low = jnp.where(iota((1, 128), 1) < 64, low.astype(f32), 0.0).astype(bf16)
         return jnp.concatenate([high, low], axis=0)
 
+    for i in range(7, 18):
+        fetches[i].wait()
     pair_t[...] = forward_form(pair_ref[1])
     own_raw = stacked(features)
     table1[:, 0:256] = side_by_side(dense(forward_form(pair_ref[0]), own_raw))
@@ -234,10 +257,10 @@
     self_rows = jnp.broadcast_to(self_ref[...].reshape(1, LAT), (16, LAT))
     self_row = dense(weight_form(self_rows), own_raw)[0:1]
     zeros64 = jnp.zeros((64, LAT), f32)
-    first_t = jnp.concatenate([jnp.transpose(tensor_ref[...]), jnp.transpose(gate1_ref[...])], axis=0)
+    first_t = jnp.concatenate([tensor_ref[...], gate1_ref[...]], axis=0)
     first_form[...] = weight_form(first_t)
     first_back[...] = forward_form(first_t)
-    gate2_t = jnp.transpose(gate2_ref[...])
+    gate2_t = gate2_ref[...]
     gate2_form[...] = weight_form(gate2_t)
     gate2_back[...] = forward_form(jnp.concatenate([gate2_t, zeros64], axis=0))
     for d in range(3):
@@ -614,15 +637,20 @@
 
 
 def per_device(grid, *args):
+    args = list(args)
+    for i in (11, 12, 15):
+        args[i] = args[i].T
+    counts, sources = args[2:4], args[:2] + args[4:]
     vmem = pl.BlockSpec(memory_space=pltpu.VMEM)
     smem = pl.BlockSpec(memory_space=pltpu.SMEM)
-    specs = [vmem] * len(args)
-    specs[2] = specs[3] = smem
+    specs = [smem] * 2 + [pl.BlockSpec(memory_space=pltpu.HBM)] * 18
     packs = [
         [pltpu.VMEM((plan[k][1], 128), f32) for k in range(8)] for plan in (PACK_ONE, PACK_TWO)
     ]
     small = [pltpu.VMEM((8, 128), f32)]
-    scratch = packs[0] * 2 + packs[1] * 4 + small * 8 + small * 2
+    scratch = [pltpu.VMEM(source.shape, source.dtype) for source in sources]
+    scratch += [pltpu.SemaphoreType.DMA((18,))]
+    scratch += packs[0] * 2 + packs[1] * 4 + small * 8 + small * 2
     scratch += [
         pltpu.VMEM((1024, EDGES), bf16),
         pltpu.VMEM((2 * EDGES, 512), bf16),
@@ -666,9 +694,9 @@
         out_specs=(vmem, vmem),
         scratch_shapes=scratch,
         compiler_params=pltpu.CompilerParams(
-            collective_id=0, has_side_effects=True, vmem_limit_bytes=48 * 1024 * 1024
+            collective_id=0, has_side_effects=True, vmem_limit_bytes=64 * 1024 * 1024
         ),
-    )(*args)
+    )(*counts, *sources)
 
 
 def solution(mesh):

time: 65.5 us -> 55.9 us (0.85)
  local copies, waits for them, and re-layouts: 11.9 us -> 1.8 us
  Pallas kernels: 51 us -> 52 us
    unnamed x35 -> x6, local copies, waits for them, and re-layouts: 11.9 us -> 1.8 us
    pallas_call x1, Pallas kernels: 51 us -> 52 us  [per_device(): pl.pallas_call(functools.partial(body, grid), out_shape=(jax.ShapeDtypeSt...]
where the time goes in v1:
time: 55.9 us; the launch traced here: 55.7 us
  Pallas kernels  52 us (93%)
  between operations  1.95 us (3%)
  local copies, waits for them, and re-layouts  1.8 us (3%)
    pallas_call x1, Pallas kernels, per_device(): pl.pallas_call(functools.partial(body, grid), out_shape=(jax.ShapeDtypeSt...  52 us
    unnamed x6, local copies, waits for them, and re-layouts  1.8 us

profile of v1, /device:TPU:1, one launch (start us, length us, event | category | flops | bytes accessed | tf_op | source)
XLA Modules:
  0.0 55.7 jit_solution(15386528217180614943)
XLA Ops:
  1.9 52.0 %shard_map.203 = (f32[3,1,1,128]{3,2,1,0:T(1,128)}, f32[1,1,128]{2,1,0:T(1,128)}) custom-call(s32[1,1]{1,0:T(1,128)S(6)} %copy.24.atom_count_ref, s32[1,1]{1,0:T(1,128)S(6)} %copy.25.edge_count_ref, f32[3,1,1,128]{3,2,1,0:T(1,128)} %refs_0_.1, f32[1,1,128,128]{3,2,1,0:T(8,128)} %refs_1_.1, s32[1,1,512]{2,1,0:T(1,128)} %refs_2_.1, s32[1,1,512]{2,1,0:T(1,128)} %refs_3_.1, ...), custom_call_target="tpu_custom_call" | custom-call | tf_op jit(solution)/shard_map/pallas_call | solution.py:687
  53.9 0.0 copy-start
  53.9 0.7 %copy-done = f32[3,1,1,128]{3,2,1,0:T(1,128)S(1)} copy-done((f32[3,1,1,128]{3,2,1,0:T(1,128)S(1)}, f32[3,1,1,128]{3,2,1,0:T(1,128)}, u32[]{:S(2)}) %copy-start) | copy-done | bytes 1560
  54.6 0.0 copy-start.1
  54.6 0.6 %copy.26 = f32[3,1,1,128]{3,2,1,0:T(1,128)} copy(f32[3,1,1,128]{3,2,1,0:T(1,128)S(1)} %copy-done) | data formatting | bytes 3072
  55.1 0.1 copy-done.1
  55.2 0.5 copy.27
Async XLA Ops:
  53.9 0.7 %copy-start = (f32[3,1,1,128]{3,2,1,0:T(1,128)S(1)}, f32[3,1,1,128]{3,2,1,0:T(1,128)}, u32[]{:S(2)}) copy-start(f32[3,1,1,128]{3,2,1,0:T(1,128)} %get-tuple-element.4) | copy-start | bytes 4612
  54.6 0.6 %copy-start.1 = (f32[1,1,128]{2,1,0:T(1,128)S(1)}, f32[1,1,128]{2,1,0:T(1,128)}, u32[]{:S(2)}) copy-start(f32[1,1,128]{2,1,0:T(1,128)} %get-tuple-element.5) | copy-start | bytes 1540

commit v2 on v1

--- a/solution.py
+++ b/solution.py
@@ -26,6 +26,8 @@
 PACK_TWO = ((2, 288), (2, 288), (8, 72), (8, 72), (24, 24), (24, 24), (24, 24), (24, 24))
 
 
+MEMBERS = (range(5), range(5, 9))
+FARTHEST_FIRST = (4, 5, 6, 7, 0, 1, 2, 3)
 FETCH_FIRST = (0, 1, 4, 5, 6)
 
 
@@ -80,26 +82,21 @@
 
 def body(
     grid,
-    atom_count_ref, edge_count_ref, *refs,
+    *refs,
 ):
-    sources, (force_ref, energy_ref), scratch = refs[:18], refs[18:20], refs[20:]
+    sources, (force_ref, energy_ref), scratch = refs[:20], refs[20:22], refs[22:]
     scratch = list(scratch)
 
     (
         pos_ref, feat_ref, centre_ref, neigh_ref, across_ref, along_ref, corner_ref, radial_ref,
         pair_ref, tensor_ref, gate1_ref, mix_ref, latent1_ref, gate2_ref, latent2_ref, readout_ref,
-        vector_ref, self_ref, fetch_sem,
-    ) = scratch[:19]
+        vector_ref, self_ref, atom_count_ref, edge_count_ref, fetch_sem,
+    ) = scratch[:21]
     fetches = [
         pltpu.make_async_copy(source, target, fetch_sem.at[i])
-        for i, (source, target) in enumerate(zip(sources, scratch[:18]))
+        for i, (source, target) in enumerate(zip(sources, scratch[:20]))
     ]
-    for i in FETCH_FIRST:
-        fetches[i].start()
-    for i in range(18):
-        if i not in FETCH_FIRST:
-            fetches[i].start()
-    del scratch[:19]
+    del scratch[:21]
 
     def take(count):
         taken = scratch[:count]
@@ -123,12 +120,11 @@
     size_x, size_y = grid
     ix, iy = lax.axis_index("gx"), lax.axis_index("gy")
 
+    along_x = {0: ix, 1: lax.rem(ix + 1, size_x), -1: lax.rem(ix + (size_x - 1), size_x)}
+    along_y = {0: iy, 1: lax.rem(iy + 1, size_y), -1: lax.rem(iy + (size_y - 1), size_y)}
+
     def device(step, sign):
-        dx, dy = step
-        return (
-            lax.rem(ix + (sign * dx + size_x), size_x),
-            lax.rem(iy + (sign * dy + size_y), size_y),
-        )
+        return along_x[sign * step[0]], along_y[sign * step[1]]
 
     still = lax.div(ix, size_x)
 
@@ -136,17 +132,23 @@
         return lat[pl.ds(pl.multiple_of(still * 8, 8) + first, 128)]
 
     barrier = pltpu.get_barrier_semaphore()
-    for step in STEPS:
+    for step in STEPS[::-1]:
         pl.semaphore_signal(
             barrier, inc=1, device_id=device(step, 1), device_id_type=pl.DeviceIdType.MESH
         )
-
-    def copy(phase, k, source, target, sign):
+    for i in FETCH_FIRST:
+        fetches[i].start()
+    for i in range(20):
+        if i not in FETCH_FIRST:
+            fetches[i].start()
+
+    def copy(phase, k, source, target, sign, slot=None):
+        slot = k if slot is None else slot
         return pltpu.make_async_remote_copy(
             src_ref=source,
             dst_ref=target,
-            send_sem=send_sem.at[phase, k],
-            recv_sem=recv_sem.at[phase, k],
+            send_sem=send_sem.at[phase, slot],
+            recv_sem=recv_sem.at[phase, slot],
             device_id=device(STEPS[k], sign),
             device_id_type=pl.DeviceIdType.MESH,
         )
@@ -185,6 +187,29 @@
 
     for i in FETCH_FIRST:
         fetches[i].wait()
+
+    def x_copies(phase, source, target, sign, chunk):
+        rows = pl.ds(144 * chunk, 144)
+        return [
+            copy(phase, k, source[k].at[rows], target[k].at[rows], sign, k + 8 * chunk) for k in range(2)
+        ]
+
+    def pack_x(table, target, chunk):
+        at = lane[:1]
+        top, bottom = table[0:144], table[144:288]
+        rows = slice(144 * chunk, 144 * chunk + 144)
+        target[0][rows] = jnp.where(at < 64, top, rolled(bottom, 64))
+        target[1][rows] = jnp.where(at < 64, rolled(top, 64), bottom)
+
+    def unpack_x_chunk(ins, chunk):
+        at = lane[:1]
+        rows = slice(144 * chunk, 144 * chunk + 144)
+        low, high = ins[0][rows], ins[1][rows]
+        top = jnp.where(at < 64, low, rolled(high, 64))
+        bottom = jnp.where(at < 64, rolled(low, 64), high)
+        return jnp.concatenate([top, bottom], axis=0)
+
+    half_rows = (slice(0, 288), slice(288, 576))
 
     across, along, corner = across_ref[0, 0], along_ref[0, 0], corner_ref[0, 0]
     list_x = jnp.concatenate([across[1:2], across[0:1]], axis=1)
@@ -214,7 +239,7 @@
         pack(PACK_ONE, k, sent[:, 0:128] if k < 2 else sent[:, 128:256], out1[k])
 
     pl.semaphore_wait(barrier, 8)
-    first_copies = [copy(0, k, out1[k], in1[k], 1) for k in range(8)]
+    first_copies = [copy(0, k, out1[k], in1[k], 1) for k in FARTHEST_FIRST]
     for one in first_copies:
         one.start()
 
@@ -248,7 +273,7 @@
         low = jnp.where(iota((1, 128), 1) < 64, low.astype(f32), 0.0).astype(bf16)
         return jnp.concatenate([high, low], axis=0)
 
-    for i in range(7, 18):
+    for i in range(7, 20):
         fetches[i].wait()
     pair_t[...] = forward_form(pair_ref[1])
     own_raw = stacked(features)
@@ -279,6 +304,8 @@
     radial_form[...] = forward_form(radial_full)
     radial_back[...] = weight_form(radial_full[:16])
 
+    lat[768:896] = mm(table1[:, 0:512], hcn[0:512])
+
     for one in first_copies:
         one.wait()
     table_x, table_s = unpack_x(PACK_ONE, in1), unpack_s(PACK_ONE, in1)
@@ -311,7 +338,7 @@
     inverse = 1.0 / length
     unit = moved * inverse
     ux, uy, uz = unit[0:1], unit[1:2], unit[2:3]
-    live = (iota((1, EDGES), 1) < edge_count_ref[0, 0]).astype(f32)
+    live = (iota((1, EDGES), 1) < edge_count_ref[...]).astype(f32)
     falloff = 1.0 / (1.0 + 0.25 * length * length)
     envelope = live * falloff
     square = ux * ux + uy * uy + uz * uz
@@ -327,7 +354,8 @@
     scaled = (length - mid_points) / WIDTH
     basis = jnp.exp(-(scaled * scaled))
     basis_full = jnp.concatenate([basis, jnp.zeros((120, EDGES), f32)], axis=0)
-    before0 = dense(radial_form[...], stacked(basis_full)) + mm(table1[...], hcn[...])
+    before0 = dense(radial_form[...], stacked(basis_full)) + lat_rows(768)
+    before0 = before0 + mm(table1[:, 512:1024], hcn[512:1024])
     latent0, slope0 = sigmoid_parts(before0)
     lat[0:128] = slope0
     lat[128:256] = latent0
@@ -348,30 +376,37 @@
         wide[row : row + 16, lanes_at(t)] = high
         wide[row : row + 16, lanes_at(t + 4)] = low
 
-    def spread(source, row0):
+    def spread(source, row0, members):
         def tile(t, carry):
             at = lanes_at(t)
             weight = 0.5 * geo[72:73, at]
             for c in range(4):
                 gate = source[row0 + 16 * c : row0 + 16 * c + 16, at] * weight
-                for m in range(9):
+                for m in members:
                     value = gate if m == 0 else gate * shape_at(m, at)
                     write_wide(64 * m + 16 * c, t, value)
             return carry
 
         lax.fori_loop(0, 4, tile, 0)
 
-    spread(grads, 64)
-    environment = mm(wide[...], hcnt[:, 0:128])
-    env_pair = side_by_side(environment)
-    table2[:, 256:512] = env_pair
-    sent = mm(env_pair, sel[...])
-    second_copies = [copy(1, k, out2[k], in2[k], 1) for k in range(8)]
-    for k in range(8):
-        pack(PACK_TWO, k, sent[:, 0:128] if k < 2 else sent[:, 128:256], out2[k])
-        second_copies[k].start()
-
-    g1[...] = mm(env_pair, hcn[0:256])
+    second_x, sent = [], []
+    second_copies = [copy(1, k, out2[k], in2[k], 1) for k in range(2, 8)]
+    for c in range(2):
+        spread(grads, 64, MEMBERS[c])
+        env_pair = side_by_side(mm(wide[half_rows[c]], hcnt[:, 0:128]))
+        table2[half_rows[c], 256:512] = env_pair
+        sent.append(mm(env_pair, sel[...]))
+        if c == 1:
+            rest = jnp.concatenate([part[:, 128:256] for part in sent], axis=0)
+            for k in (4, 5, 6, 7, 2, 3):
+                pack(PACK_TWO, k, rest, out2[k])
+                second_copies[k - 2].start()
+        pack_x(sent[c][:, 0:128], out2, c)
+        second_x.append(x_copies(1, out2, in2, 1, c))
+        for one in second_x[c]:
+            one.start()
+
+    g1[...] = mm(table2[:, 256:512], hcn[0:256])
 
     def couple(t, carry):
         at = lanes_at(t)
@@ -408,41 +443,49 @@
     latent1 = lat_rows(128) + act1
     lat[384:512] = latent1
     high1, low1 = split(latent1)
-    pile[0:128] = high1
-    pile[384:512] = low1
+    early = jnp.concatenate([latent2_form[:, 0:128], latent2_form[:, 384:512]], axis=1)
+    lat[896:1024] = dense(early, jnp.concatenate([high1, low1], axis=0))
     grads[128:192] = dense(gate2_form[...], jnp.concatenate([high1, low1], axis=0))
-    spread(grads, 128)
+    spread(grads, 128, range(9))
     table2[:, 0:256] = side_by_side(mm(wide[...], hcnt[:, 0:128]))
-    joint[...] = mm(table2[:, 0:512], hcn[0:512])
+    joint[...] = mm(table2[...], hcn[0:512])
     for m in range(9):
         t1[64 * m : 64 * m + 64] = dense(mix_form[DEGREE[m]], mixed[m])
 
-    for k in range(2):
-        second_copies[k].wait()
-    table2[:, 512:768] = side_by_side(unpack_x(PACK_TWO, in2))
-    for k in range(2, 8):
-        second_copies[k].wait()
-    table2[:, 768:1024] = side_by_side(unpack_s(PACK_TWO, in2))
-    joint[...] += mm(table2[:, 512:1024], hcn[512:1024])
-
-    def contract(t, carry):
-        at = lanes_at(t)
-        for c in range(4):
-            sums = [None, None, None]
-            for m in range(9):
-                row = 64 * m + 16 * c
-                term = t1[row : row + 16, at] * joint[row : row + 16, at]
-                d = DEGREE[m]
-                sums[d] = term if sums[d] is None else sums[d] + term
-            for d in range(3):
-                high, low = split(sums[d])
-                row = 128 + 64 * d + 16 * c
-                pile[row : row + 16, at] = high
-                pile[384 + row : 400 + row, at] = low
-        return carry
-
-    lax.fori_loop(0, 4, contract, 0)
-    act2, slope2 = sigmoid_parts(dense(latent2_form[...], pile[...]))
+    for one in second_x[0]:
+        one.wait()
+    joint[0:288] += mm(side_by_side(unpack_x_chunk(in2, 0)), hcn[512:768])
+    for one in second_copies:
+        one.wait()
+    joint[...] += mm(side_by_side(unpack_s(PACK_TWO, in2)), hcn[768:1024])
+
+    def contract(degrees):
+        def tile(t, carry):
+            at = lanes_at(t)
+            for c in range(4):
+                for d in degrees:
+                    total = None
+                    for m in range(9):
+                        if DEGREE[m] == d:
+                            row = 64 * m + 16 * c
+                            term = t1[row : row + 16, at] * joint[row : row + 16, at]
+                            total = term if total is None else total + term
+                    high, low = split(total)
+                    row = 128 + 64 * d + 16 * c
+                    pile[row : row + 16, at] = high
+                    pile[384 + row : 400 + row, at] = low
+            return carry
+
+        lax.fori_loop(0, 4, tile, 0)
+
+    contract((0, 1))
+    for one in second_x[1]:
+        one.wait()
+    joint[288:576] += mm(side_by_side(unpack_x_chunk(in2, 1)), hcn[512:768])
+    contract((2,))
+    late = jnp.concatenate([latent2_form[:, 128:384], latent2_form[:, 512:768]], axis=1)
+    late_pile = jnp.concatenate([pile[128:384], pile[512:768]], axis=0)
+    act2, slope2 = sigmoid_parts(lat_rows(896) + dense(late, late_pile))
     latent2 = lat_rows(384) + act2
     hidden, slope_h = sigmoid_parts(dense(readout_form[...], stacked(latent2)))
     vector_wide = jnp.concatenate([vector_col[...]] * 4, axis=1)
@@ -455,21 +498,32 @@
     lat[512:640] = d_latent2 + d_pile[0:128]
     grads[192:384] = d_pile[128:320]
 
-    def joint_back(t, carry):
-        at = lanes_at(t)
-        for c in range(4):
-            d_sum = [grads[192 + 64 * d + 16 * c : 208 + 64 * d + 16 * c, at] for d in range(3)]
-            for m in range(9):
-                row = 64 * m + 16 * c
-                write_wide(row, t, t1[row : row + 16, at] * d_sum[DEGREE[m]])
-        return carry
-
-    lax.fori_loop(0, 4, joint_back, 0)
-    back = mm(wide[...], hcnt[:, 256:512])
-    third_copies = [copy(2, k, out3[k], in3[k], -1) for k in range(8)]
-    for k in range(8):
-        pack(PACK_TWO, k, back[:, 0:128] if k < 2 else back[:, 128:256], out3[k])
-        third_copies[k].start()
+    def joint_back(members):
+        def tile(t, carry):
+            at = lanes_at(t)
+            for c in range(4):
+                d_sum = [grads[192 + 64 * d + 16 * c : 208 + 64 * d + 16 * c, at] for d in range(3)]
+                for m in members:
+                    row = 64 * m + 16 * c
+                    write_wide(row, t, t1[row : row + 16, at] * d_sum[DEGREE[m]])
+            return carry
+
+        lax.fori_loop(0, 4, tile, 0)
+
+    third_x, sent = [], []
+    third_copies = [copy(2, k, out3[k], in3[k], -1) for k in range(2, 8)]
+    for c in range(2):
+        joint_back(MEMBERS[c])
+        sent.append(mm(wide[half_rows[c]], hcnt[:, 256:512]))
+        if c == 1:
+            rest = jnp.concatenate([part[:, 128:256] for part in sent], axis=0)
+            for k in (4, 5, 6, 7, 2, 3):
+                pack(PACK_TWO, k, rest, out3[k])
+                third_copies[k - 2].start()
+        pack_x(sent[c][:, 0:128], out3, c)
+        third_x.append(x_copies(2, out3, in3, -1, c))
+        for one in third_x[c]:
+            one.start()
 
     back = mm(wide[...], hcnt[:, 0:256])
     env_own[...] = back[:, 128:256]
@@ -584,13 +638,17 @@
     lax.fori_loop(0, 4, couple_back, 0)
     env_own[...] += mm(wide[...], hcnt[:, 0:128])
 
+    for one in third_x[0]:
+        one.wait()
+    env_own[0:288] += mm(side_by_side(unpack_x_chunk(in3, 0)), selt[0:256])
     for one in third_copies:
         one.wait()
-    ghosts = jnp.concatenate(
-        [side_by_side(unpack_x(PACK_TWO, in3)), side_by_side(unpack_s(PACK_TWO, in3))], axis=1
-    )
-    d_environment = env_own[...] + mm(ghosts, selt[...])
-    big[...] = mm(side_by_side(d_environment), hcn[0:256])
+    env_own[...] += mm(side_by_side(unpack_s(PACK_TWO, in3)), selt[256:512])
+    big[0:288] = mm(side_by_side(env_own[0:288]), hcn[0:256])
+    for one in third_x[1]:
+        one.wait()
+    d_environment = env_own[288:576] + mm(side_by_side(unpack_x_chunk(in3, 1)), selt[0:256])
+    big[288:576] = mm(side_by_side(d_environment), hcn[0:256])
     spread_back(grads, 64, 512, False)
     d_latent0 = lat_rows(640) + dense(first_back[...], stacked(grads[448:576]))
     d_basis = dense(radial_back[...], stacked(d_latent0 * lat_rows(0)))[:8]
@@ -615,13 +673,13 @@
     d_centre = halves(mm(d_parts, hcnt[0:EDGES, 0:128]))
     out4[0][...] = d_table[:, 128:256]
     out4[1][...] = d_table[:, 256:384]
-    last_copies = [copy(3, k, out4[0] if k < 2 else out4[1], in4[k], -1) for k in range(8)]
+    last_copies = [copy(3, k, out4[0] if k < 2 else out4[1], in4[k], -1) for k in FARTHEST_FIRST]
     for one in last_copies:
         one.start()
     d_own = d_table[:, 0:128] - d_centre
 
     per_atom = halves(mm(folded(jnp.broadcast_to(edge_energy, (8, EDGES))), hcnt[0:EDGES, 0:128]))[0:1]
-    alive = (iota((1, ATOMS), 1) < atom_count_ref[0, 0]).astype(f32)
+    alive = (iota((1, ATOMS), 1) < atom_count_ref[...]).astype(f32)
     energy_ref[0] = alive * (per_atom + self_row)
 
     for one in last_copies:
@@ -640,16 +698,15 @@
     args = list(args)
     for i in (11, 12, 15):
         args[i] = args[i].T
-    counts, sources = args[2:4], args[:2] + args[4:]
+    sources = args[:2] + args[4:] + args[2:4]
     vmem = pl.BlockSpec(memory_space=pltpu.VMEM)
-    smem = pl.BlockSpec(memory_space=pltpu.SMEM)
-    specs = [smem] * 2 + [pl.BlockSpec(memory_space=pltpu.HBM)] * 18
+    specs = [pl.BlockSpec(memory_space=pltpu.HBM)] * 20
     packs = [
         [pltpu.VMEM((plan[k][1], 128), f32) for k in range(8)] for plan in (PACK_ONE, PACK_TWO)
     ]
     small = [pltpu.VMEM((8, 128), f32)]
     scratch = [pltpu.VMEM(source.shape, source.dtype) for source in sources]
-    scratch += [pltpu.SemaphoreType.DMA((18,))]
+    scratch += [pltpu.SemaphoreType.DMA((20,))]
     scratch += packs[0] * 2 + packs[1] * 4 + small * 8 + small * 2
     scratch += [
         pltpu.VMEM((1024, EDGES), bf16),
@@ -657,9 +714,9 @@
         pltpu.VMEM((256, 256), bf16),
         pltpu.VMEM((512, 128), bf16),
         pltpu.VMEM((128, 1024), bf16),
-        pltpu.VMEM((576, 1024), bf16),
+        pltpu.VMEM((576, 512), bf16),
         pltpu.VMEM((80, EDGES), f32),
-        pltpu.VMEM((768, EDGES), f32),
+        pltpu.VMEM((1024, EDGES), f32),
         pltpu.VMEM((576, EDGES), f32),
         pltpu.VMEM((576, EDGES), f32),
         pltpu.VMEM((576, EDGES), f32),
@@ -681,8 +738,8 @@
         pltpu.VMEM((256, 256), bf16),
         pltpu.VMEM((32, 256), bf16),
         pltpu.VMEM((256, EDGES), bf16),
-        pltpu.SemaphoreType.DMA((4, 8)),
-        pltpu.SemaphoreType.DMA((4, 8)),
+        pltpu.SemaphoreType.DMA((4, 10)),
+        pltpu.SemaphoreType.DMA((4, 10)),
     ]
     return pl.pallas_call(
         functools.partial(body, grid),
@@ -696,7 +753,7 @@
         compiler_params=pltpu.CompilerParams(
             collective_id=0, has_side_effects=True, vmem_limit_bytes=64 * 1024 * 1024
         ),
-    )(*counts, *sources)
+    )(*sources)
 
 
 def solution(mesh):

time: 55.9 us -> 52 us (0.930)
  Pallas kernels: 52 us -> 48.1 us
    pallas_call x1, Pallas kernels: 52 us -> 48.1 us  [per_device(): pl.pallas_call(functools.partial(body, grid), out_shape=(jax.ShapeDtypeSt...]
where the time goes in v2:
time: 52 us; the launch traced here: 51.9 us
  Pallas kernels  48.1 us (92%)
  between operations  1.95 us (4%)
  local copies, waits for them, and re-layouts  1.8 us (3%)
    pallas_call x1, Pallas kernels, per_device(): pl.pallas_call(functools.partial(body, grid), out_shape=(jax.ShapeDtypeSt...  48.1 us
    unnamed x6, local copies, waits for them, and re-layouts  1.8 us

profile of v2, /device:TPU:1, one launch (start us, length us, event | category | flops | bytes accessed | tf_op | source)
XLA Modules:
  0.0 51.9 jit_solution(16574213188100047370)
XLA Ops:
  1.9 48.1 %shard_map.203 = (f32[3,1,1,128]{3,2,1,0:T(1,128)}, f32[1,1,128]{2,1,0:T(1,128)}) custom-call(f32[3,1,1,128]{3,2,1,0:T(1,128)} %refs_0_.1, f32[1,1,128,128]{3,2,1,0:T(8,128)} %refs_1_.1, s32[1,1,512]{2,1,0:T(1,128)} %refs_2_.1, s32[1,1,512]{2,1,0:T(1,128)} %refs_3_.1, s32[1,1,2,64]{3,2,1,0:T(2,128)} %refs_4_.1, s32[1,1,2,16]{3,2,1,0:T(2,128)} %refs_5_.1, ...), custom_call_target="tpu_custom_call" | custom-call | tf_op jit(solution)/shard_map/pallas_call | solution.py:744
  50.1 0.0 copy-start
  50.1 0.7 %copy-done = f32[3,1,1,128]{3,2,1,0:T(1,128)S(1)} copy-done((f32[3,1,1,128]{3,2,1,0:T(1,128)S(1)}, f32[3,1,1,128]{3,2,1,0:T(1,128)}, u32[]{:S(2)}) %copy-start) | copy-done | bytes 1560
  50.7 0.0 copy-start.1
  50.7 0.6 %copy.26 = f32[3,1,1,128]{3,2,1,0:T(1,128)} copy(f32[3,1,1,128]{3,2,1,0:T(1,128)S(1)} %copy-done) | data formatting | bytes 3072
  51.3 0.1 copy-done.1
  51.4 0.5 copy.27
Async XLA Ops:
  50.1 0.7 %copy-start = (f32[3,1,1,128]{3,2,1,0:T(1,128)S(1)}, f32[3,1,1,128]{3,2,1,0:T(1,128)}, u32[]{:S(2)}) copy-start(f32[3,1,1,128]{3,2,1,0:T(1,128)} %get-tuple-element.4) | copy-start | bytes 4612
  50.7 0.6 %copy-start.1 = (f32[1,1,128]{2,1,0:T(1,128)S(1)}, f32[1,1,128]{2,1,0:T(1,128)}, u32[]{:S(2)}) copy-start(f32[1,1,128]{2,1,0:T(1,128)} %get-tuple-element.5) | copy-start | bytes 1540

commit v3 on v2

--- a/solution.py
+++ b/solution.py
@@ -26,9 +26,9 @@
 PACK_TWO = ((2, 288), (2, 288), (8, 72), (8, 72), (24, 24), (24, 24), (24, 24), (24, 24))
 
 
-MEMBERS = (range(5), range(5, 9))
+MEMBERS = (range(3), range(3, 6), range(6, 9))
 FARTHEST_FIRST = (4, 5, 6, 7, 0, 1, 2, 3)
-FETCH_FIRST = (0, 1, 4, 5, 6)
+FETCH_FIRST = (0, 1, 8, 4, 5, 6)
 
 
 def split(value):
@@ -84,7 +84,7 @@
     grid,
     *refs,
 ):
-    sources, (force_ref, energy_ref), scratch = refs[:20], refs[20:22], refs[22:]
+    sources, out_ref, scratch = refs[:20], refs[20], refs[21:]
     scratch = list(scratch)
 
     (
@@ -108,9 +108,9 @@
     (
         hcn, hcnt, sel, selt, table1, table2, geo, lat, grads, big,
         g1, t1, joint, wide, mixed, pile, acc, env_own,
-        pair_t, first_form, first_back, gate2_form, gate2_back, mix_form, mix_back, latent1_form,
+        first_form, first_back, gate2_form, gate2_back, mix_form, mix_back, latent1_form,
         latent1_back, latent2_form, latent2_back, readout_form, readout_back, vector_col,
-        radial_form, radial_back, gate_pair,
+        radial_form, radial_back, gate_pair, pair2,
     ) = take(35)
     send_sem, recv_sem = take(2)
 
@@ -189,27 +189,28 @@
         fetches[i].wait()
 
     def x_copies(phase, source, target, sign, chunk):
-        rows = pl.ds(144 * chunk, 144)
+        rows = pl.ds(96 * chunk, 96)
         return [
-            copy(phase, k, source[k].at[rows], target[k].at[rows], sign, k + 8 * chunk) for k in range(2)
+            copy(phase, k, source[k].at[rows], target[k].at[rows], sign, k if chunk == 0 else 6 + k + 2 * chunk)
+            for k in range(2)
         ]
 
     def pack_x(table, target, chunk):
         at = lane[:1]
-        top, bottom = table[0:144], table[144:288]
-        rows = slice(144 * chunk, 144 * chunk + 144)
+        top, bottom = table[0:96], table[96:192]
+        rows = slice(96 * chunk, 96 * chunk + 96)
         target[0][rows] = jnp.where(at < 64, top, rolled(bottom, 64))
         target[1][rows] = jnp.where(at < 64, rolled(top, 64), bottom)
 
     def unpack_x_chunk(ins, chunk):
         at = lane[:1]
-        rows = slice(144 * chunk, 144 * chunk + 144)
+        rows = slice(96 * chunk, 96 * chunk + 96)
         low, high = ins[0][rows], ins[1][rows]
         top = jnp.where(at < 64, low, rolled(high, 64))
         bottom = jnp.where(at < 64, rolled(low, 64), high)
         return jnp.concatenate([top, bottom], axis=0)
 
-    half_rows = (slice(0, 288), slice(288, 576))
+    third_rows = [slice(192 * c, 192 * c + 192) for c in range(3)]
 
     across, along, corner = across_ref[0, 0], along_ref[0, 0], corner_ref[0, 0]
     list_x = jnp.concatenate([across[1:2], across[0:1]], axis=1)
@@ -232,7 +233,9 @@
     pos_high = pos_own.astype(bf16).astype(f32)
     pos_mid = (pos_own - pos_high).astype(bf16).astype(f32)
     pos_low = pos_own - pos_high - pos_mid
-    raw = side_by_side(jnp.concatenate([features, pos_own, pos_low], axis=0))
+    own_raw = stacked(features)
+    projected = dense(weight_form(jnp.transpose(pair_ref[1])), own_raw)
+    raw = side_by_side(jnp.concatenate([projected, pos_own, pos_low], axis=0))
     sent = mm(raw, sel[...])
     sent = jnp.concatenate([sent[:128], sent[128:136] + sent[136:144], sent[136:144]], axis=0)
     for k in range(8):
@@ -273,12 +276,10 @@
         low = jnp.where(iota((1, 128), 1) < 64, low.astype(f32), 0.0).astype(bf16)
         return jnp.concatenate([high, low], axis=0)
 
-    for i in range(7, 20):
+    for i in (7, *range(9, 20)):
         fetches[i].wait()
-    pair_t[...] = forward_form(pair_ref[1])
-    own_raw = stacked(features)
     table1[:, 0:256] = side_by_side(dense(forward_form(pair_ref[0]), own_raw))
-    table1[:, 256:512] = side_by_side(dense(pair_t[...], own_raw))
+    table1[:, 256:512] = side_by_side(projected)
     self_rows = jnp.broadcast_to(self_ref[...].reshape(1, LAT), (16, LAT))
     self_row = dense(weight_form(self_rows), own_raw)[0:1]
     zeros64 = jnp.zeros((64, LAT), f32)
@@ -309,10 +310,8 @@
     for one in first_copies:
         one.wait()
     table_x, table_s = unpack_x(PACK_ONE, in1), unpack_s(PACK_ONE, in1)
-    ghost_raw = jnp.concatenate([table_x[:128], table_s[:128]], axis=1)
-    ghost_proj = dense(pair_t[...], stacked(ghost_raw))
-    table1[:, 512:768] = side_by_side(ghost_proj[:, 0:128])
-    table1[:, 768:1024] = side_by_side(ghost_proj[:, 128:256])
+    table1[:, 512:768] = side_by_side(table_x[:128])
+    table1[:, 768:1024] = side_by_side(table_s[:128])
 
     def offsets(rows):
         total = jnp.zeros((8, 128), f32)
@@ -391,12 +390,12 @@
 
     second_x, sent = [], []
     second_copies = [copy(1, k, out2[k], in2[k], 1) for k in range(2, 8)]
-    for c in range(2):
+    for c in range(3):
         spread(grads, 64, MEMBERS[c])
-        env_pair = side_by_side(mm(wide[half_rows[c]], hcnt[:, 0:128]))
-        table2[half_rows[c], 256:512] = env_pair
+        env_pair = side_by_side(mm(wide[third_rows[c]], hcnt[:, 0:128]))
+        table2[third_rows[c], 256:512] = env_pair
         sent.append(mm(env_pair, sel[...]))
-        if c == 1:
+        if c == 2:
             rest = jnp.concatenate([part[:, 128:256] for part in sent], axis=0)
             for k in (4, 5, 6, 7, 2, 3):
                 pack(PACK_TWO, k, rest, out2[k])
@@ -452,9 +451,10 @@
     for m in range(9):
         t1[64 * m : 64 * m + 64] = dense(mix_form[DEGREE[m]], mixed[m])
 
-    for one in second_x[0]:
-        one.wait()
-    joint[0:288] += mm(side_by_side(unpack_x_chunk(in2, 0)), hcn[512:768])
+    for c in range(2):
+        for one in second_x[c]:
+            one.wait()
+        joint[third_rows[c]] += mm(side_by_side(unpack_x_chunk(in2, c)), hcn[512:768])
     for one in second_copies:
         one.wait()
     joint[...] += mm(side_by_side(unpack_s(PACK_TWO, in2)), hcn[768:1024])
@@ -479,9 +479,9 @@
         lax.fori_loop(0, 4, tile, 0)
 
     contract((0, 1))
-    for one in second_x[1]:
+    for one in second_x[2]:
         one.wait()
-    joint[288:576] += mm(side_by_side(unpack_x_chunk(in2, 1)), hcn[512:768])
+    joint[384:576] += mm(side_by_side(unpack_x_chunk(in2, 2)), hcn[512:768])
     contract((2,))
     late = jnp.concatenate([latent2_form[:, 128:384], latent2_form[:, 512:768]], axis=1)
     late_pile = jnp.concatenate([pile[128:384], pile[512:768]], axis=0)
@@ -494,9 +494,10 @@
 
     d_hidden = vector_wide * envelope * slope_h
     d_latent2 = dense(readout_back[...], stacked(d_hidden))
-    d_pile = dense(latent2_back[...], stacked(d_latent2 * slope2))
-    lat[512:640] = d_latent2 + d_pile[0:128]
-    grads[192:384] = d_pile[128:320]
+    d_before2 = stacked(d_latent2 * slope2)
+    grads[192:384] = mm(latent2_back[128:320], d_before2) + mm(latent2_back[448:640], d_before2)
+    lat[512:640] = d_latent2
+    pair2[...] = d_before2
 
     def joint_back(members):
         def tile(t, carry):
@@ -512,10 +513,10 @@
 
     third_x, sent = [], []
     third_copies = [copy(2, k, out3[k], in3[k], -1) for k in range(2, 8)]
-    for c in range(2):
+    for c in range(3):
         joint_back(MEMBERS[c])
-        sent.append(mm(wide[half_rows[c]], hcnt[:, 256:512]))
-        if c == 1:
+        sent.append(mm(wide[third_rows[c]], hcnt[:, 256:512]))
+        if c == 2:
             rest = jnp.concatenate([part[:, 128:256] for part in sent], axis=0)
             for k in (4, 5, 6, 7, 2, 3):
                 pack(PACK_TWO, k, rest, out3[k])
@@ -525,6 +526,8 @@
         for one in third_x[c]:
             one.start()
 
+    both = mm(latent2_back[0:128], pair2[...]) + mm(latent2_back[320:448], pair2[...])
+    lat[512:640] = lat_rows(512) + both
     back = mm(wide[...], hcnt[:, 0:256])
     env_own[...] = back[:, 128:256]
     big[...] = mm(side_by_side(back[:, 0:128]), hcn[0:256])
@@ -547,7 +550,7 @@
     def halves(value):
         return value[0:8] + value[8:16]
 
-    def spread_back(source, row0, target0, fresh):
+    def spread_back(source, row0, target0, members, fresh, first, last):
         def tile(t, carry):
             at = lanes_at(t)
             half = 0.5 * geo[72:73, at]
@@ -556,33 +559,34 @@
             for c in range(4):
                 gate = source[row0 + 16 * c : row0 + 16 * c + 16, at]
                 weight = gate * half
-                total = None
-                for m in range(9):
+                total = None if first else grads[target0 + 16 * c : target0 + 16 * c + 16, at]
+                for m in members:
                     row = 64 * m + 16 * c
                     value = big[row : row + 16, at]
                     if m:
                         term = halves(value * weight)
                         d_shape[m] = term if c == 0 else d_shape[m] + term
                         value = value * shape_at(m, at)
-                    total = value if m == 0 else total + value
-                grads[target0 + 16 * c : target0 + 16 * c + 16, at] = total * half
-                term = halves(total * gate)
-                d_env = term if c == 0 else d_env + term
-            d_env = 0.5 * d_env
-            for m in range(1, 9):
-                if fresh:
+                    total = value if total is None else total + value
+                if last:
+                    term = halves(total * gate)
+                    d_env = term if c == 0 else d_env + term
+                    total = total * half
+                grads[target0 + 16 * c : target0 + 16 * c + 16, at] = total
+            for m in members:
+                if m and fresh:
                     acc[drow(m) : drow(m) + 8, at] = d_shape[m]
-                else:
+                elif m:
                     acc[drow(m) : drow(m) + 8, at] += d_shape[m]
-            if fresh:
-                acc[0:8, at] = d_env
-            else:
-                acc[0:8, at] += d_env
+            if last and fresh:
+                acc[0:8, at] = 0.5 * d_env
+            elif last:
+                acc[0:8, at] += 0.5 * d_env
             return carry
 
         lax.fori_loop(0, 4, tile, 0)
 
-    spread_back(grads, 128, 384, True)
+    spread_back(grads, 128, 384, range(9), True, True, True)
     gate_high, gate_low = split(grads[384:448])
     gate_pair[0:64] = gate_high
     gate_pair[64:128] = nothing
@@ -638,18 +642,20 @@
     lax.fori_loop(0, 4, couple_back, 0)
     env_own[...] += mm(wide[...], hcnt[:, 0:128])
 
-    for one in third_x[0]:
-        one.wait()
-    env_own[0:288] += mm(side_by_side(unpack_x_chunk(in3, 0)), selt[0:256])
+    for c in range(2):
+        for one in third_x[c]:
+            one.wait()
+        env_own[third_rows[c]] += mm(side_by_side(unpack_x_chunk(in3, c)), selt[0:256])
     for one in third_copies:
         one.wait()
     env_own[...] += mm(side_by_side(unpack_s(PACK_TWO, in3)), selt[256:512])
-    big[0:288] = mm(side_by_side(env_own[0:288]), hcn[0:256])
-    for one in third_x[1]:
+    big[0:384] = mm(side_by_side(env_own[0:384]), hcn[0:256])
+    spread_back(grads, 64, 512, range(6), False, True, False)
+    for one in third_x[2]:
         one.wait()
-    d_environment = env_own[288:576] + mm(side_by_side(unpack_x_chunk(in3, 1)), selt[0:256])
-    big[288:576] = mm(side_by_side(d_environment), hcn[0:256])
-    spread_back(grads, 64, 512, False)
+    d_environment = env_own[384:576] + mm(side_by_side(unpack_x_chunk(in3, 2)), selt[0:256])
+    big[384:576] = mm(side_by_side(d_environment), hcn[0:256])
+    spread_back(grads, 64, 512, range(6, 9), False, False, True)
     d_latent0 = lat_rows(640) + dense(first_back[...], stacked(grads[448:576]))
     d_basis = dense(radial_back[...], stacked(d_latent0 * lat_rows(0)))[:8]
     d_length = jnp.sum(d_basis * basis * scaled, axis=0, keepdims=True) * (-2.0 / WIDTH)
@@ -680,7 +686,7 @@
 
     per_atom = halves(mm(folded(jnp.broadcast_to(edge_energy, (8, EDGES))), hcnt[0:EDGES, 0:128]))[0:1]
     alive = (iota((1, ATOMS), 1) < atom_count_ref[...]).astype(f32)
-    energy_ref[0] = alive * (per_atom + self_row)
+    out_ref[3, 0] = -(alive * (per_atom + self_row))
 
     for one in last_copies:
         one.wait()
@@ -691,7 +697,7 @@
     returned = mm(folded(grad_x), selt[0:128]) + mm(folded(grad_s), selt[256:384])
     total = d_own + halves(returned)
     for axis in range(3):
-        force_ref[axis, 0] = -total[axis : axis + 1]
+        out_ref[axis, 0] = total[axis : axis + 1]
 
 
 def per_device(grid, *args):
@@ -730,7 +736,7 @@
         *(
             pltpu.VMEM(shape, bf16)
             for shape in (
-                (256, 256), (256, 256), (256, 256), (128, 256), (256, 256), (3, 128, 128),
+                (256, 256), (256, 256), (128, 256), (256, 256), (3, 128, 128),
                 (3, 128, 128), (256, 768), (640, 256), (256, 768), (640, 256), (256, 256), (256, 256),
             )
         ),
@@ -738,22 +744,22 @@
         pltpu.VMEM((256, 256), bf16),
         pltpu.VMEM((32, 256), bf16),
         pltpu.VMEM((256, EDGES), bf16),
-        pltpu.SemaphoreType.DMA((4, 10)),
-        pltpu.SemaphoreType.DMA((4, 10)),
+        pltpu.VMEM((256, EDGES), bf16),
+        pltpu.SemaphoreType.DMA((4, 12)),
+        pltpu.SemaphoreType.DMA((4, 12)),
     ]
-    return pl.pallas_call(
+    result = pl.pallas_call(
         functools.partial(body, grid),
-        out_shape=(
-            jax.ShapeDtypeStruct((3, 1, 1, ATOMS), f32),
-            jax.ShapeDtypeStruct((1, 1, ATOMS), f32),
-        ),
+        out_shape=jax.ShapeDtypeStruct((4, 1, 1, ATOMS), f32),
         in_specs=specs,
-        out_specs=(vmem, vmem),
+        out_specs=vmem,
         scratch_shapes=scratch,
         compiler_params=pltpu.CompilerParams(
             collective_id=0, has_side_effects=True, vmem_limit_bytes=64 * 1024 * 1024
         ),
     )(*sources)
+    result = -result
+    return result[:3], result[3]
 
 
 def solution(mesh):

time: 52 us -> 51.6 us (level)
  local copies, waits for them, and re-layouts: 1.8 us -> 1.08 us
  other arithmetic: 0 us -> 0.69 us
    unnamed x6 -> x0, local copies, waits for them, and re-layouts: 1.8 us -> none
    neg x0 -> x1, other arithmetic: none -> 0.69 us  [per_device(): result = -result]
    slice x0 -> x1, local copies, waits for them, and re-layouts: none -> 0.56 us  [per_device(): return (result[:3], result[3])]
where the time goes in v3:
time: 51.6 us; the launch traced here: 51.4 us
  Pallas kernels  47.7 us (92%)
  between operations  1.94 us (4%)
  local copies, waits for them, and re-layouts  1.08 us (2%)
  other arithmetic  0.69 us (1%)
    pallas_call x1, Pallas kernels, per_device(): pl.pallas_call(functools.partial(body, grid), out_shape=jax.ShapeDtypeStr...  47.7 us

profile of v3, /device:TPU:1, one launch (start us, length us, event | category | flops | bytes accessed | tf_op | source)
XLA Modules:
  0.0 51.4 jit_solution(2663449249919801125)
XLA Ops:
  1.9 47.7 %shard_map.203 = f32[4,1,1,128]{3,2,1,0:T(1,128)} custom-call(f32[3,1,1,128]{3,2,1,0:T(1,128)} %refs_0_.1, f32[1,1,128,128]{3,2,1,0:T(8,128)} %refs_1_.1, s32[1,1,512]{2,1,0:T(1,128)} %refs_2_.1, s32[1,1,512]{2,1,0:T(1,128)} %refs_3_.1, s32[1,1,2,64]{3,2,1,0:T(2,128)} %refs_4_.1, s32[1,1,2,16]{3,2,1,0:T(2,128)} %refs_5_.1, s32[1,1,4,4]{3,2,1,0:T(4,128)} %refs_6_.1, ...), custom_call_target="tpu_custom_call" | custom-call | tf_op jit(solution)/shard_map/pallas_call | solution.py:751
  49.7 0.7 %neg.3 = f32[4,1,1,128]{3,2,1,0:T(1,128)S(1)} negate(f32[4,1,1,128]{3,2,1,0:T(1,128)} %shard_map.203) | non-fusion elementwise | flops 512 | bytes 4096 | tf_op jit(solution)/shard_map/neg | solution.py:761
  50.3 0.5 slice_bitcast_fusion
  50.9 0.6 %slice.8 = f32[3,1,1,128]{3,2,1,0:T(1,128)} slice(f32[4,1,1,128]{3,2,1,0:T(1,128)S(1)} %neg.3), slice={[0:3], [0:1], [0:1], [0:128]} | slice | bytes 3072 | tf_op jit(solution)/shard_map/slice | solution.py:762

commit v4 on v3

--- a/solution.py
+++ b/solution.py
@@ -110,8 +110,8 @@
         g1, t1, joint, wide, mixed, pile, acc, env_own,
         first_form, first_back, gate2_form, gate2_back, mix_form, mix_back, latent1_form,
         latent1_back, latent2_form, latent2_back, readout_form, readout_back, vector_col,
-        radial_form, radial_back, gate_pair, pair2,
-    ) = take(35)
+        radial_form, radial_back, gate_pair, pair2, edge_sel, edge_selt,
+    ) = take(37)
     send_sem, recv_sem = take(2)
 
     def drow(m):
@@ -266,6 +266,14 @@
     for t in range(2):
         selt[256 * t : 256 * t + 128] = selt_f[128 * t : 128 * t + 128]
         selt[256 * t + 128 : 256 * t + 256] = selt_f[128 * t : 128 * t + 128]
+
+    picked = mm(hot_ct, chosen).astype(bf16)
+    edge_sel[0:EDGES] = picked
+    edge_sel[EDGES : 2 * EDGES] = picked
+    returned_hot = mm(selt_f, hot_c).astype(bf16)
+    for t in range(2):
+        edge_selt[256 * t : 256 * t + 128] = returned_hot[128 * t : 128 * t + 128]
+        edge_selt[256 * t + 128 : 256 * t + 256] = returned_hot[128 * t : 128 * t + 128]
 
     def forward_form(weight):
         return weight_form(jnp.transpose(weight))
@@ -307,11 +315,14 @@
 
     lat[768:896] = mm(table1[:, 0:512], hcn[0:512])
 
-    for one in first_copies:
+    for one in first_copies[4:6]:
         one.wait()
-    table_x, table_s = unpack_x(PACK_ONE, in1), unpack_s(PACK_ONE, in1)
-    table1[:, 512:768] = side_by_side(table_x[:128])
-    table1[:, 768:1024] = side_by_side(table_s[:128])
+    table_x = unpack_x(PACK_ONE, in1)
+    lat[768:896] = lat_rows(768) + mm(side_by_side(table_x[:128]), hcn[512:768])
+    for one in first_copies[:4] + first_copies[6:]:
+        one.wait()
+    table_s = unpack_s(PACK_ONE, in1)
+    table1[:, 512:768] = side_by_side(table_s[:128])
 
     def offsets(rows):
         total = jnp.zeros((8, 128), f32)
@@ -354,7 +365,7 @@
     basis = jnp.exp(-(scaled * scaled))
     basis_full = jnp.concatenate([basis, jnp.zeros((120, EDGES), f32)], axis=0)
     before0 = dense(radial_form[...], stacked(basis_full)) + lat_rows(768)
-    before0 = before0 + mm(table1[:, 512:1024], hcn[512:1024])
+    before0 = before0 + mm(table1[:, 512:768], hcn[768:1024])
     latent0, slope0 = sigmoid_parts(before0)
     lat[0:128] = slope0
     lat[128:256] = latent0
@@ -392,9 +403,7 @@
     second_copies = [copy(1, k, out2[k], in2[k], 1) for k in range(2, 8)]
     for c in range(3):
         spread(grads, 64, MEMBERS[c])
-        env_pair = side_by_side(mm(wide[third_rows[c]], hcnt[:, 0:128]))
-        table2[third_rows[c], 256:512] = env_pair
-        sent.append(mm(env_pair, sel[...]))
+        sent.append(mm(wide[third_rows[c]], edge_sel[...]))
         if c == 2:
             rest = jnp.concatenate([part[:, 128:256] for part in sent], axis=0)
             for k in (4, 5, 6, 7, 2, 3):
@@ -405,6 +414,7 @@
         for one in second_x[c]:
             one.start()
 
+    table2[:, 256:512] = side_by_side(mm(wide[...], hcnt[:, 0:128]))
     g1[...] = mm(table2[:, 256:512], hcn[0:256])
 
     def couple(t, carry):
@@ -479,12 +489,15 @@
         lax.fori_loop(0, 4, tile, 0)
 
     contract((0, 1))
+    part = jnp.concatenate([latent2_form[:, 128:256], latent2_form[:, 512:640]], axis=1)
+    part_pile = jnp.concatenate([pile[128:256], pile[512:640]], axis=0)
+    lat[896:1024] = lat_rows(896) + dense(part, part_pile)
     for one in second_x[2]:
         one.wait()
     joint[384:576] += mm(side_by_side(unpack_x_chunk(in2, 2)), hcn[512:768])
     contract((2,))
-    late = jnp.concatenate([latent2_form[:, 128:384], latent2_form[:, 512:768]], axis=1)
-    late_pile = jnp.concatenate([pile[128:384], pile[512:768]], axis=0)
+    late = jnp.concatenate([latent2_form[:, 256:384], latent2_form[:, 640:768]], axis=1)
+    late_pile = jnp.concatenate([pile[256:384], pile[640:768]], axis=0)
     act2, slope2 = sigmoid_parts(lat_rows(896) + dense(late, late_pile))
     latent2 = lat_rows(384) + act2
     hidden, slope_h = sigmoid_parts(dense(readout_form[...], stacked(latent2)))
@@ -642,19 +655,18 @@
     lax.fori_loop(0, 4, couple_back, 0)
     env_own[...] += mm(wide[...], hcnt[:, 0:128])
 
+    big[...] = mm(side_by_side(env_own[...]), hcn[0:256])
     for c in range(2):
         for one in third_x[c]:
             one.wait()
-        env_own[third_rows[c]] += mm(side_by_side(unpack_x_chunk(in3, c)), selt[0:256])
+        big[third_rows[c]] += mm(side_by_side(unpack_x_chunk(in3, c)), edge_selt[0:256])
     for one in third_copies:
         one.wait()
-    env_own[...] += mm(side_by_side(unpack_s(PACK_TWO, in3)), selt[256:512])
-    big[0:384] = mm(side_by_side(env_own[0:384]), hcn[0:256])
+    big[...] += mm(side_by_side(unpack_s(PACK_TWO, in3)), edge_selt[256:512])
     spread_back(grads, 64, 512, range(6), False, True, False)
     for one in third_x[2]:
         one.wait()
-    d_environment = env_own[384:576] + mm(side_by_side(unpack_x_chunk(in3, 2)), selt[0:256])
-    big[384:576] = mm(side_by_side(d_environment), hcn[0:256])
+    big[384:576] += mm(side_by_side(unpack_x_chunk(in3, 2)), edge_selt[0:256])
     spread_back(grads, 64, 512, range(6, 9), False, False, True)
     d_latent0 = lat_rows(640) + dense(first_back[...], stacked(grads[448:576]))
     d_basis = dense(radial_back[...], stacked(d_latent0 * lat_rows(0)))[:8]
@@ -719,7 +731,7 @@
         pltpu.VMEM((2 * EDGES, 512), bf16),
         pltpu.VMEM((256, 256), bf16),
         pltpu.VMEM((512, 128), bf16),
-        pltpu.VMEM((128, 1024), bf16),
+        pltpu.VMEM((128, 768), bf16),
         pltpu.VMEM((576, 512), bf16),
         pltpu.VMEM((80, EDGES), f32),
         pltpu.VMEM((1024, EDGES), f32),
@@ -745,6 +757,8 @@
         pltpu.VMEM((32, 256), bf16),
         pltpu.VMEM((256, EDGES), bf16),
         pltpu.VMEM((256, EDGES), bf16),
+        pltpu.VMEM((2 * EDGES, 256), bf16),
+        pltpu.VMEM((512, EDGES), bf16),
         pltpu.SemaphoreType.DMA((4, 12)),
         pltpu.SemaphoreType.DMA((4, 12)),
     ]

time: 51.6 us -> 51.4 us (level)
  no operation moved by 1% of the time
where the time goes in v4:
time: 51.4 us; the launch traced here: 51.2 us
  Pallas kernels  47.5 us (92%)
  between operations  1.94 us (4%)
  local copies, waits for them, and re-layouts  1.08 us (2%)
  other arithmetic  0.69 us (1%)
    pallas_call x1, Pallas kernels, per_device(): pl.pallas_call(functools.partial(body, grid), out_shape=jax.ShapeDtypeStr...  47.5 us

profile of v4, /device:TPU:1, one launch (start us, length us, event | category | flops | bytes accessed | tf_op | source)
XLA Modules:
  0.0 51.2 jit_solution(11715883089847425204)
XLA Ops:
  1.9 47.5 %shard_map.203 = f32[4,1,1,128]{3,2,1,0:T(1,128)} custom-call(f32[3,1,1,128]{3,2,1,0:T(1,128)} %refs_0_.1, f32[1,1,128,128]{3,2,1,0:T(8,128)} %refs_1_.1, s32[1,1,512]{2,1,0:T(1,128)} %refs_2_.1, s32[1,1,512]{2,1,0:T(1,128)} %refs_3_.1, s32[1,1,2,64]{3,2,1,0:T(2,128)} %refs_4_.1, s32[1,1,2,16]{3,2,1,0:T(2,128)} %refs_5_.1, s32[1,1,4,4]{3,2,1,0:T(4,128)} %refs_6_.1, ...), custom_call_target="tpu_custom_call" | custom-call | tf_op jit(solution)/shard_map/pallas_call | solution.py:765
  49.5 0.7 %neg.3 = f32[4,1,1,128]{3,2,1,0:T(1,128)S(1)} negate(f32[4,1,1,128]{3,2,1,0:T(1,128)} %shard_map.203) | non-fusion elementwise | flops 512 | bytes 4096 | tf_op jit(solution)/shard_map/neg | solution.py:775
  50.2 0.5 %slice_bitcast_fusion = f32[1,1,128]{2,1,0:T(1,128)} fusion(f32[4,1,1,128]{3,2,1,0:T(1,128)S(1)} %neg.3), kind=kLoop, calls=%fused_computation | loop fusion | bytes 1024 | tf_op jit(solution)/shard_map/squeeze | solution.py:776
  50.7 0.6 %slice.8 = f32[3,1,1,128]{3,2,1,0:T(1,128)} slice(f32[4,1,1,128]{3,2,1,0:T(1,128)S(1)} %neg.3), slice={[0:3], [0:1], [0:1], [0:128]} | slice | bytes 3072 | tf_op jit(solution)/shard_map/slice | solution.py:776
